TPU v7x, 256 devices: a whole 4x4x8 slice. The times are simulated.
256 devices in a mesh: dp: 16 (over x, z_hi, core), seq: 16 (over y, z_lo).
Axes of the slice: x: 4, y: 4, z: 8 (z_hi: 2, z_lo: 4; z = z_hi * 4 + z_lo), core: 2. Of those that a mesh axis runs over, the one named last changes fastest.
Arguments:
- tokens: bfloat16 [16, 2048, 1536], P('dp', 'seq'), may hold values from -8 to 8
- lengths: int32 [16], P('dp'), may hold values from 512 to 2048
- cotangent: bfloat16 [16, 2048, 1536], P('dp', 'seq'), may hold values from -6 to 6
- gain: float32 [1536], replicated, may hold values from 0.25 to 1.75
- w_q: bfloat16 [1536, 512], replicated, may hold values from -1 to 1
- w_kv: bfloat16 [1536, 320], replicated, may hold values from -1 to 1
- w_o: bfloat16 [768, 1536], replicated, may hold values from -0.21875 to 0.21875
Outputs:
- grad_tokens: bfloat16 [16, 2048, 1536], P('dp', 'seq')
- grad_wq: float32 [1536, 512], P(('dp', 'seq'))
- grad_wkv: float32 [1536, 320], P(('dp', 'seq'))
- grad_wo_t: float32 [1536, 768], P(('dp', 'seq'))
All inputs are finite; a program needn't handle non-finite values.
Results may differ from a plain program's by a relative error of at most 0.034.
Values may be sent and summed in bfloat16 or wider, within the bound.
A program may use at most 128 MiB of HBM per device.

v0:
```python
import jax
import jax.numpy as jnp
from jax import lax
from jax.sharding import PartitionSpec as P

HK = 128


EPS = 1e-06


def body(tokens, lengths, cotangent, gain, w_q, w_kv, w_o):
    head_k = HK
    head_v = w_kv.shape[1] - head_k
    heads = w_q.shape[1] // head_k
    scale = head_k ** (-0.5)
    xtok = tokens[0]
    grad_out = cotangent[0]
    length = lengths[0]
    xf = xtok.astype(jnp.float32)
    rscale = lax.rsqrt(jnp.mean(xf * xf, axis=-1, keepdims=True) + EPS)
    normed = (xf * rscale * gain).astype(jnp.bfloat16)
    query = jnp.dot(normed, w_q, preferred_element_type=jnp.float32).astype(jnp.bfloat16)
    local_kv = jnp.dot(normed, w_kv, preferred_element_type=jnp.float32).astype(jnp.bfloat16)
    keyval = lax.all_gather(local_kv, "seq", axis=0, tiled=True)
    keys = keyval[:, :head_k]
    vals = keyval[:, head_k:]
    total_keys = keyval.shape[0]
    valid = jnp.arange(total_keys, dtype=jnp.int32)[None, :] < length
    d_att = jnp.dot(grad_out, w_o.T, preferred_element_type=jnp.float32).astype(jnp.bfloat16)
    outs = []
    dqs = []
    d_key = jnp.zeros((total_keys, head_k), jnp.float32)
    d_val = jnp.zeros((total_keys, head_v), jnp.float32)
    for head in range(heads):
        q_head = query[:, head * head_k : (head + 1) * head_k]
        da_head = d_att[:, head * head_v : (head + 1) * head_v]
        scores = jnp.dot(q_head, keys.T, preferred_element_type=jnp.float32) * scale
        scores = jnp.where(valid, scores, -1e30)
        top = jnp.max(scores, axis=-1, keepdims=True)
        expo = jnp.exp(scores - top)
        prob = expo / jnp.sum(expo, axis=-1, keepdims=True)
        prob_b = prob.astype(jnp.bfloat16)
        att = jnp.dot(prob_b, vals, preferred_element_type=jnp.float32).astype(jnp.bfloat16)
        delta = jnp.sum(
            da_head.astype(jnp.float32) * att.astype(jnp.float32), axis=-1, keepdims=True
        )
        dpv = jnp.dot(da_head, vals.T, preferred_element_type=jnp.float32)
        d_score = (prob * (dpv - delta) * scale).astype(jnp.bfloat16)
        dqs.append(jnp.dot(d_score, keys, preferred_element_type=jnp.float32).astype(jnp.bfloat16))
        d_key = d_key + jnp.dot(d_score.T, q_head, preferred_element_type=jnp.float32)
        d_val = d_val + jnp.dot(prob_b.T, da_head, preferred_element_type=jnp.float32)
        outs.append(att)
    attended = jnp.concatenate(outs, axis=1)
    d_query = jnp.concatenate(dqs, axis=1)
    key_terms = jnp.concatenate([d_key, d_val], axis=1)
    d_keyval = lax.psum_scatter(
        key_terms.astype(jnp.bfloat16), "seq", scatter_dimension=0, tiled=True
    )
    part_q = jnp.dot(normed.T, d_query, preferred_element_type=jnp.float32)
    part_kv = jnp.dot(normed.T, d_keyval, preferred_element_type=jnp.float32)
    part_o = jnp.dot(grad_out.T, attended, preferred_element_type=jnp.float32)
    grad_wq, grad_wkv, grad_wo_t = (
        lax.psum_scatter(part_q, ("dp", "seq"), scatter_dimension=0, tiled=True),
        lax.psum_scatter(part_kv, ("dp", "seq"), scatter_dimension=0, tiled=True),
        lax.psum_scatter(part_o, ("dp", "seq"), scatter_dimension=0, tiled=True),
    )
    d_normed = jnp.dot(d_query, w_q.T, preferred_element_type=jnp.float32) + jnp.dot(
        d_keyval, w_kv.T, preferred_element_type=jnp.float32
    )
    inner = jnp.mean(xf * gain * d_normed, axis=-1, keepdims=True)
    grad_x = grad_out.astype(jnp.float32) + rscale * gain * d_normed - xf * rscale**3 * inner
    return (grad_x.astype(jnp.bfloat16)[None], grad_wq, grad_wkv, grad_wo_t)


def solution(mesh):
    return jax.shard_map(
        body,
        mesh=mesh,
        in_specs=(P("dp", "seq", None), P("dp"), P("dp", "seq", None), P(), P(), P(), P()),
        out_specs=(
            P("dp", "seq", None),
            P(("dp", "seq"), None),
            P(("dp", "seq"), None),
            P(("dp", "seq"), None),
        ),
        check_vma=False,
    )
```

profile of v0, /device:TPU:1, one launch (start us, length us, event | category | flops | bytes accessed | tf_op | source)
XLA Modules:
  0.0 1432.0 jit_solution(12346255668299306661)
XLA Ops:
  8.6 2.5 convolution_convert_fusion.2
  11.8 1.8 convolution_convert_fusion.1
  14.6 66.4 %all-gather.2.cloned.1.call-done = bf16[2048,320]{0,1:T(8,128)(2,1)} async-done(((bf16[128,320]{0,1:T(8,128)(2,1)}), bf16[2048,320]{0,1:T(8,128)(2,1)}) %all-gather.2.cloned.1.call-update) | async-done | bytes 1310736 | tf_op jit(solution)/shard_map/all_gather | solution.py:25
  80.9 1.5 fusion.107
  94.5 2.5 copy.25
  97.1 1.6 convolution_convert_fusion.7
  98.8 1.5 convolution_convert_fusion.9
  100.3 1.4 convolution_convert_fusion.8
  102.1 3.0 convolution_bitcast_fusion
  105.1 77.5 %reduce-scatter.7.cloned.1.call-done = bf16[128,320]{1,0:T(8,128)(2,1)} async-done(((bf16[2048,320]{1,0:T(8,128)(2,1)}), bf16[128,320]{1,0:T(8,128)(2,1)}) %reduce-scatter.7.cloned.1.call-update) | async-done | bytes 81936
  182.6 2.9 fusion.91
  185.5 2.5 fusion.87
  188.0 646.7 %fusion = f32[8,512]{1,0:T(8,128)S(1)} fusion(f32[1536,512]{1,0:T(8,128)} %fusion.87), kind=kCustom, calls=%all-reduce-scatter | all-reduce-scatter fusion | flops 1048577 | bytes 3162112
  834.7 1.4 collective-permute-start.62
  841.4 18.1 %collective-permute-start.58 = (f32[8,512]{1,0:T(8,128)S(1)}, f32[8,512]{1,0:T(8,128)S(1)}, u32[]{:S(2)}, u32[]{:S(2)}) collective-permute-start(f32[8,512]{1,0:T(8,128)S(1)} %fusion), channel_id=1, source_target_pairs={{0,59},{1,60},{2,61},{3,62},{4,63},{5,64},{6,65},{7,66},{8,67},{9,... | collective-permute-start | bytes 49160
  859.5 28.5 %collective-permute-start.57 = (f32[8,512]{1,0:T(8,128)S(1)}, f32[8,512]{1,0:T(8,128)S(1)}, u32[]{:S(2)}, u32[]{:S(2)}) collective-permute-start(f32[8,512]{1,0:T(8,128)S(1)} %fusion), channel_id=1, source_target_pairs={{0,58},{1,59},{2,60},{3,61},{4,62},{5,63},{6,64},{7,65},{8,66},{9,... | collective-permute-start | bytes 49160
  888.0 1.9 collective-permute-start.56
  890.0 1.9 collective-permute-start.55
  905.1 10.0 collective-permute-start.44
  915.1 4.2 collective-permute-start.43
  920.6 3.5 collective-permute-start.41
  924.1 4.4 collective-permute-start.40
  928.6 2.8 collective-permute-start.39
  934.0 2.3 collective-permute-start.36
  936.3 4.7 collective-permute-start.35
  942.4 1.8 collective-permute-start.33
  944.2 2.0 collective-permute-start.32
  946.3 2.9 collective-permute-start.31
  949.2 3.0 collective-permute-start.30
  952.2 4.2 collective-permute-start.29
  956.4 4.0 collective-permute-start.28
  960.5 3.5 collective-permute-start.27
  964.0 13.1 collective-permute-start.26
  977.2 13.1 collective-permute-start.25
  990.3 13.1 collective-permute-start.24
  1003.5 13.1 collective-permute-start.23
  1016.6 13.1 collective-permute-start.22
  1029.8 13.1 collective-permute-start.21
  1042.9 13.1 collective-permute-start.20
  1056.1 13.1 collective-permute-start.19
  1069.2 13.1 collective-permute-start.18
  1082.4 13.1 collective-permute-start.17
  1095.5 13.1 collective-permute-start.16
  1108.7 13.1 collective-permute-start.15
  1121.9 13.1 collective-permute-start.14
  1135.0 13.1 collective-permute-start.13
  1148.2 13.1 collective-permute-start.12
  1161.3 13.1 collective-permute-start.11
  1174.4 13.1 collective-permute-start.10
  1187.6 13.1 collective-permute-start.9
  1200.7 13.1 collective-permute-start.8
  1213.9 13.1 collective-permute-start.7
  1227.0 13.1 collective-permute-start.6
  1240.2 13.1 collective-permute-start.5
  1253.3 13.1 collective-permute-start.4
  1266.4 13.1 collective-permute-start.3
  1279.6 13.1 collective-permute-start.2
  1292.7 13.1 collective-permute-start.1
  1305.9 13.1 collective-permute-start
  1319.4 7.5 collective-permute-done
  1326.9 90.2 %concatenate.13 = f32[518,512]{1,0:T(8,128)} concatenate(f32[6,512]{1,0:T(8,128)S(1)} %collective-permute-done.63, f32[8,512]{1,0:T(8,128)S(1)} %collective-permute-done.62, f32[8,512]{1,0:T(8,128)S(1)} %collective-permute-done.61, f32[8,512]{1,0:T(8,128)S(1)} %collective-permute-done.60, f32[8,512]{1,0:T(8,128)S(1)} %collective-permute-done.59, ...), dimensions={0} | concatenate | bytes 2121728
  1417.1 1.5 constant_dynamic-slice_fusion
  1418.6 1.6 fusion.108
  1422.0 1.3 constant_dynamic-slice_fusion.1
  (237 shorter events, 42.1 us)
Async XLA Ops:
  7.2 73.7 %all-gather.2.cloned.1.call-start = ((), (), s32[]{:S(2)}) async-start(), calls=%async_computation.1 | async-start | bytes 1392640 | tf_op jit(solution)/shard_map/all_gather | solution.py:25
  11.1 171.5 %reduce-scatter.7.cloned.1.call-start = ((), (), s32[]{:S(2)}) async-start(), calls=%async_computation.2 | async-start | bytes 1671168
  97.0 1325.0 %all-reduce.7.cloned.1.call-start = ((), (), s32[]{:S(2)}) async-start(), calls=%async_computation.3 | async-start | bytes 14155776
  834.7 24.8 %collective-permute-start.62 = (f32[8,512]{1,0:T(8,128)S(1)}, f32[8,512]{1,0:T(8,128)S(1)}, u32[]{:S(2)}, u32[]{:S(2)}) collective-permute-start(f32[8,512]{1,0:T(8,128)S(1)} %fusion), channel_id=1, source_target_pairs={{0,63},{1,64},{2,65},{3,66},{4,67},{5,68},{6,69},{7,70},{8,71},{9,... | collective-permute-start | bytes 49160
  836.2 51.9 %collective-permute-start.61 = (f32[8,512]{1,0:T(8,128)S(1)}, f32[8,512]{1,0:T(8,128)S(1)}, u32[]{:S(2)}, u32[]{:S(2)}) collective-permute-start(f32[8,512]{1,0:T(8,128)S(1)} %fusion), channel_id=1, source_target_pairs={{0,62},{1,63},{2,64},{3,65},{4,66},{5,67},{6,68},{7,69},{8,70},{9,... | collective-permute-start | bytes 49160
  837.5 52.5 %collective-permute-start.60 = (f32[8,512]{1,0:T(8,128)S(1)}, f32[8,512]{1,0:T(8,128)S(1)}, u32[]{:S(2)}, u32[]{:S(2)}) collective-permute-start(f32[8,512]{1,0:T(8,128)S(1)} %fusion), channel_id=1, source_target_pairs={{0,61},{1,62},{2,63},{3,64},{4,65},{5,66},{6,67},{7,68},{8,69},{9,... | collective-permute-start | bytes 49160
  840.1 51.8 %collective-permute-start.59 = (f32[8,512]{1,0:T(8,128)S(1)}, f32[8,512]{1,0:T(8,128)S(1)}, u32[]{:S(2)}, u32[]{:S(2)}) collective-permute-start(f32[8,512]{1,0:T(8,128)S(1)} %fusion), channel_id=1, source_target_pairs={{0,60},{1,61},{2,62},{3,63},{4,64},{5,65},{6,66},{7,67},{8,68},{9,... | collective-permute-start | bytes 49160
  841.4 51.8 %collective-permute-start.58 = (f32[8,512]{1,0:T(8,128)S(1)}, f32[8,512]{1,0:T(8,128)S(1)}, u32[]{:S(2)}, u32[]{:S(2)}) collective-permute-start(f32[8,512]{1,0:T(8,128)S(1)} %fusion), channel_id=1, source_target_pairs={{0,59},{1,60},{2,61},{3,62},{4,63},{5,64},{6,65},{7,66},{8,67},{9,... | collective-permute-start | bytes 49160
  859.5 35.0 %collective-permute-start.57 = (f32[8,512]{1,0:T(8,128)S(1)}, f32[8,512]{1,0:T(8,128)S(1)}, u32[]{:S(2)}, u32[]{:S(2)}) collective-permute-start(f32[8,512]{1,0:T(8,128)S(1)} %fusion), channel_id=1, source_target_pairs={{0,58},{1,59},{2,60},{3,61},{4,62},{5,63},{6,64},{7,65},{8,66},{9,... | collective-permute-start | bytes 49160
  888.0 7.8 collective-permute-start.56
  890.0 7.2 collective-permute-start.55
  894.5 6.6 collective-permute-start.52
  895.8 6.6 collective-permute-start.51
  897.1 6.6 collective-permute-start.50
  898.5 6.6 collective-permute-start.49
  899.8 15.3 %collective-permute-start.48 = (f32[8,512]{1,0:T(8,128)S(1)}, f32[8,512]{1,0:T(8,128)S(1)}, u32[]{:S(2)}, u32[]{:S(2)}) collective-permute-start(f32[8,512]{1,0:T(8,128)S(1)} %fusion), channel_id=1, source_target_pairs={{0,49},{1,50},{2,51},{3,52},{4,53},{5,54},{6,55},{7,56},{8,57},{9,... | collective-permute-start | bytes 49160
  901.1 18.2 %collective-permute-start.47 = (f32[8,512]{1,0:T(8,128)S(1)}, f32[8,512]{1,0:T(8,128)S(1)}, u32[]{:S(2)}, u32[]{:S(2)}) collective-permute-start(f32[8,512]{1,0:T(8,128)S(1)} %fusion), channel_id=1, source_target_pairs={{0,48},{1,49},{2,50},{3,51},{4,52},{5,53},{6,54},{7,55},{8,56},{9,... | collective-permute-start | bytes 49160
  902.4 18.2 %collective-permute-start.46 = (f32[8,512]{1,0:T(8,128)S(1)}, f32[8,512]{1,0:T(8,128)S(1)}, u32[]{:S(2)}, u32[]{:S(2)}) collective-permute-start(f32[8,512]{1,0:T(8,128)S(1)} %fusion), channel_id=1, source_target_pairs={{0,47},{1,48},{2,49},{3,50},{4,51},{5,52},{6,53},{7,54},{8,55},{9,... | collective-permute-start | bytes 49160
  903.8 20.4 %collective-permute-start.45 = (f32[8,512]{1,0:T(8,128)S(1)}, f32[8,512]{1,0:T(8,128)S(1)}, u32[]{:S(2)}, u32[]{:S(2)}) collective-permute-start(f32[8,512]{1,0:T(8,128)S(1)} %fusion), channel_id=1, source_target_pairs={{0,46},{1,47},{2,48},{3,49},{4,50},{5,51},{6,52},{7,53},{8,54},{9,... | collective-permute-start | bytes 49160
  905.1 23.5 %collective-permute-start.44 = (f32[8,512]{1,0:T(8,128)S(1)}, f32[8,512]{1,0:T(8,128)S(1)}, u32[]{:S(2)}, u32[]{:S(2)}) collective-permute-start(f32[8,512]{1,0:T(8,128)S(1)} %fusion), channel_id=1, source_target_pairs={{0,45},{1,46},{2,47},{3,48},{4,49},{5,50},{6,51},{7,52},{8,53},{9,... | collective-permute-start | bytes 49160
  915.1 16.3 %collective-permute-start.43 = (f32[8,512]{1,0:T(8,128)S(1)}, f32[8,512]{1,0:T(8,128)S(1)}, u32[]{:S(2)}, u32[]{:S(2)}) collective-permute-start(f32[8,512]{1,0:T(8,128)S(1)} %fusion), channel_id=1, source_target_pairs={{0,44},{1,45},{2,46},{3,47},{4,48},{5,49},{6,50},{7,51},{8,52},{9,... | collective-permute-start | bytes 49160
  919.3 13.4 collective-permute-start.42
  920.6 13.4 collective-permute-start.41
  924.1 12.2 collective-permute-start.40
  928.6 12.5 collective-permute-start.39
  931.4 11.0 collective-permute-start.38
  932.7 11.5 collective-permute-start.37
  934.0 12.2 collective-permute-start.36
  936.3 12.8 collective-permute-start.35
  941.1 11.1 collective-permute-start.34
  942.4 14.0 collective-permute-start.33
  944.2 16.3 %collective-permute-start.32 = (f32[8,512]{1,0:T(8,128)S(1)}, f32[8,512]{1,0:T(8,128)S(1)}, u32[]{:S(2)}, u32[]{:S(2)}) collective-permute-start(f32[8,512]{1,0:T(8,128)S(1)} %fusion), channel_id=1, source_target_pairs={{0,33},{1,34},{2,35},{3,36},{4,37},{5,38},{6,39},{7,40},{8,41},{9,... | collective-permute-start | bytes 49160
  946.3 17.8 %collective-permute-start.31 = (f32[8,512]{1,0:T(8,128)S(1)}, f32[8,512]{1,0:T(8,128)S(1)}, u32[]{:S(2)}, u32[]{:S(2)}) collective-permute-start(f32[8,512]{1,0:T(8,128)S(1)} %fusion), channel_id=1, source_target_pairs={{0,32},{1,33},{2,34},{3,35},{4,36},{5,37},{6,38},{7,39},{8,40},{9,... | collective-permute-start | bytes 49160
  949.2 28.0 %collective-permute-start.30 = (f32[8,512]{1,0:T(8,128)S(1)}, f32[8,512]{1,0:T(8,128)S(1)}, u32[]{:S(2)}, u32[]{:S(2)}) collective-permute-start(f32[8,512]{1,0:T(8,128)S(1)} %fusion), channel_id=1, source_target_pairs={{0,31},{1,32},{2,33},{3,34},{4,35},{5,36},{6,37},{7,38},{8,39},{9,... | collective-permute-start | bytes 49160
  952.2 38.1 %collective-permute-start.29 = (f32[8,512]{1,0:T(8,128)S(1)}, f32[8,512]{1,0:T(8,128)S(1)}, u32[]{:S(2)}, u32[]{:S(2)}) collective-permute-start(f32[8,512]{1,0:T(8,128)S(1)} %fusion), channel_id=1, source_target_pairs={{0,30},{1,31},{2,32},{3,33},{4,34},{5,35},{6,36},{7,37},{8,38},{9,... | collective-permute-start | bytes 49160
  956.4 47.0 %collective-permute-start.28 = (f32[8,512]{1,0:T(8,128)S(1)}, f32[8,512]{1,0:T(8,128)S(1)}, u32[]{:S(2)}, u32[]{:S(2)}) collective-permute-start(f32[8,512]{1,0:T(8,128)S(1)} %fusion), channel_id=1, source_target_pairs={{0,29},{1,30},{2,31},{3,32},{4,33},{5,34},{6,35},{7,36},{8,37},{9,... | collective-permute-start | bytes 49160
  960.5 56.1 %collective-permute-start.27 = (f32[8,512]{1,0:T(8,128)S(1)}, f32[8,512]{1,0:T(8,128)S(1)}, u32[]{:S(2)}, u32[]{:S(2)}) collective-permute-start(f32[8,512]{1,0:T(8,128)S(1)} %fusion), channel_id=1, source_target_pairs={{0,28},{1,29},{2,30},{3,31},{4,32},{5,33},{6,34},{7,35},{8,36},{9,... | collective-permute-start | bytes 49160
  964.0 65.7 %collective-permute-start.26 = (f32[8,512]{1,0:T(8,128)S(1)}, f32[8,512]{1,0:T(8,128)S(1)}, u32[]{:S(2)}, u32[]{:S(2)}) collective-permute-start(f32[8,512]{1,0:T(8,128)S(1)} %fusion), channel_id=1, source_target_pairs={{0,27},{1,28},{2,29},{3,30},{4,31},{5,32},{6,33},{7,34},{8,35},{9,... | collective-permute-start | bytes 49160
  977.2 65.7 %collective-permute-start.25 = (f32[8,512]{1,0:T(8,128)S(1)}, f32[8,512]{1,0:T(8,128)S(1)}, u32[]{:S(2)}, u32[]{:S(2)}) collective-permute-start(f32[8,512]{1,0:T(8,128)S(1)} %fusion), channel_id=1, source_target_pairs={{0,26},{1,27},{2,28},{3,29},{4,30},{5,31},{6,32},{7,33},{8,34},{9,... | collective-permute-start | bytes 49160
  990.3 65.7 %collective-permute-start.24 = (f32[8,512]{1,0:T(8,128)S(1)}, f32[8,512]{1,0:T(8,128)S(1)}, u32[]{:S(2)}, u32[]{:S(2)}) collective-permute-start(f32[8,512]{1,0:T(8,128)S(1)} %fusion), channel_id=1, source_target_pairs={{0,25},{1,26},{2,27},{3,28},{4,29},{5,30},{6,31},{7,32},{8,33},{9,... | collective-permute-start | bytes 49160
  1003.5 65.7 %collective-permute-start.23 = (f32[8,512]{1,0:T(8,128)S(1)}, f32[8,512]{1,0:T(8,128)S(1)}, u32[]{:S(2)}, u32[]{:S(2)}) collective-permute-start(f32[8,512]{1,0:T(8,128)S(1)} %fusion), channel_id=1, source_target_pairs={{0,24},{1,25},{2,26},{3,27},{4,28},{5,29},{6,30},{7,31},{8,32},{9,... | collective-permute-start | bytes 49160
  1016.6 65.7 %collective-permute-start.22 = (f32[8,512]{1,0:T(8,128)S(1)}, f32[8,512]{1,0:T(8,128)S(1)}, u32[]{:S(2)}, u32[]{:S(2)}) collective-permute-start(f32[8,512]{1,0:T(8,128)S(1)} %fusion), channel_id=1, source_target_pairs={{0,23},{1,24},{2,25},{3,26},{4,27},{5,28},{6,29},{7,30},{8,31},{9,... | collective-permute-start | bytes 49160
  1029.8 65.7 %collective-permute-start.21 = (f32[8,512]{1,0:T(8,128)S(1)}, f32[8,512]{1,0:T(8,128)S(1)}, u32[]{:S(2)}, u32[]{:S(2)}) collective-permute-start(f32[8,512]{1,0:T(8,128)S(1)} %fusion), channel_id=1, source_target_pairs={{0,22},{1,23},{2,24},{3,25},{4,26},{5,27},{6,28},{7,29},{8,30},{9,... | collective-permute-start | bytes 49160
  1042.9 65.7 %collective-permute-start.20 = (f32[8,512]{1,0:T(8,128)S(1)}, f32[8,512]{1,0:T(8,128)S(1)}, u32[]{:S(2)}, u32[]{:S(2)}) collective-permute-start(f32[8,512]{1,0:T(8,128)S(1)} %fusion), channel_id=1, source_target_pairs={{0,21},{1,22},{2,23},{3,24},{4,25},{5,26},{6,27},{7,28},{8,29},{9,... | collective-permute-start | bytes 49160
  1056.1 65.7 %collective-permute-start.19 = (f32[8,512]{1,0:T(8,128)S(1)}, f32[8,512]{1,0:T(8,128)S(1)}, u32[]{:S(2)}, u32[]{:S(2)}) collective-permute-start(f32[8,512]{1,0:T(8,128)S(1)} %fusion), channel_id=1, source_target_pairs={{0,20},{1,21},{2,22},{3,23},{4,24},{5,25},{6,26},{7,27},{8,28},{9,... | collective-permute-start | bytes 49160
  1069.2 65.7 %collective-permute-start.18 = (f32[8,512]{1,0:T(8,128)S(1)}, f32[8,512]{1,0:T(8,128)S(1)}, u32[]{:S(2)}, u32[]{:S(2)}) collective-permute-start(f32[8,512]{1,0:T(8,128)S(1)} %fusion), channel_id=1, source_target_pairs={{0,19},{1,20},{2,21},{3,22},{4,23},{5,24},{6,25},{7,26},{8,27},{9,... | collective-permute-start | bytes 49160
  1082.4 65.7 %collective-permute-start.17 = (f32[8,512]{1,0:T(8,128)S(1)}, f32[8,512]{1,0:T(8,128)S(1)}, u32[]{:S(2)}, u32[]{:S(2)}) collective-permute-start(f32[8,512]{1,0:T(8,128)S(1)} %fusion), channel_id=1, source_target_pairs={{0,18},{1,19},{2,20},{3,21},{4,22},{5,23},{6,24},{7,25},{8,26},{9,... | collective-permute-start | bytes 49160
  1095.5 65.7 %collective-permute-start.16 = (f32[8,512]{1,0:T(8,128)S(1)}, f32[8,512]{1,0:T(8,128)S(1)}, u32[]{:S(2)}, u32[]{:S(2)}) collective-permute-start(f32[8,512]{1,0:T(8,128)S(1)} %fusion), channel_id=1, source_target_pairs={{0,17},{1,18},{2,19},{3,20},{4,21},{5,22},{6,23},{7,24},{8,25},{9,... | collective-permute-start | bytes 49160
  1108.7 65.7 %collective-permute-start.15 = (f32[8,512]{1,0:T(8,128)S(1)}, f32[8,512]{1,0:T(8,128)}, u32[]{:S(2)}, u32[]{:S(2)}) collective-permute-start(f32[8,512]{1,0:T(8,128)S(1)} %fusion), channel_id=1, source_target_pairs={{0,16},{1,17},{2,18},{3,19},{4,20},{5,21},{6,22},{7,23},{8,24},{9,... | collective-permute-start | bytes 49160
  1121.9 65.7 %collective-permute-start.14 = (f32[8,512]{1,0:T(8,128)S(1)}, f32[8,512]{1,0:T(8,128)}, u32[]{:S(2)}, u32[]{:S(2)}) collective-permute-start(f32[8,512]{1,0:T(8,128)S(1)} %fusion), channel_id=1, source_target_pairs={{0,15},{1,16},{2,17},{3,18},{4,19},{5,20},{6,21},{7,22},{8,23},{9,... | collective-permute-start | bytes 49160
  1135.0 65.7 %collective-permute-start.13 = (f32[8,512]{1,0:T(8,128)S(1)}, f32[8,512]{1,0:T(8,128)}, u32[]{:S(2)}, u32[]{:S(2)}) collective-permute-start(f32[8,512]{1,0:T(8,128)S(1)} %fusion), channel_id=1, source_target_pairs={{0,14},{1,15},{2,16},{3,17},{4,18},{5,19},{6,20},{7,21},{8,22},{9,... | collective-permute-start | bytes 49160
  1148.2 65.7 %collective-permute-start.12 = (f32[8,512]{1,0:T(8,128)S(1)}, f32[8,512]{1,0:T(8,128)}, u32[]{:S(2)}, u32[]{:S(2)}) collective-permute-start(f32[8,512]{1,0:T(8,128)S(1)} %fusion), channel_id=1, source_target_pairs={{0,13},{1,14},{2,15},{3,16},{4,17},{5,18},{6,19},{7,20},{8,21},{9,... | collective-permute-start | bytes 49160
  1161.3 65.7 %collective-permute-start.11 = (f32[8,512]{1,0:T(8,128)S(1)}, f32[8,512]{1,0:T(8,128)}, u32[]{:S(2)}, u32[]{:S(2)}) collective-permute-start(f32[8,512]{1,0:T(8,128)S(1)} %fusion), channel_id=1, source_target_pairs={{0,12},{1,13},{2,14},{3,15},{4,16},{5,17},{6,18},{7,19},{8,20},{9,... | collective-permute-start | bytes 49160
  1174.4 65.7 %collective-permute-start.10 = (f32[8,512]{1,0:T(8,128)S(1)}, f32[8,512]{1,0:T(8,128)}, u32[]{:S(2)}, u32[]{:S(2)}) collective-permute-start(f32[8,512]{1,0:T(8,128)S(1)} %fusion), channel_id=1, source_target_pairs={{0,11},{1,12},{2,13},{3,14},{4,15},{5,16},{6,17},{7,18},{8,19},{9,... | collective-permute-start | bytes 49160
  1187.6 65.7 %collective-permute-start.9 = (f32[8,512]{1,0:T(8,128)S(1)}, f32[8,512]{1,0:T(8,128)}, u32[]{:S(2)}, u32[]{:S(2)}) collective-permute-start(f32[8,512]{1,0:T(8,128)S(1)} %fusion), channel_id=1, source_target_pairs={{0,10},{1,11},{2,12},{3,13},{4,14},{5,15},{6,16},{7,17},{8,18},{9,... | collective-permute-start | bytes 49160
  1200.7 65.7 %collective-permute-start.8 = (f32[8,512]{1,0:T(8,128)S(1)}, f32[8,512]{1,0:T(8,128)}, u32[]{:S(2)}, u32[]{:S(2)}) collective-permute-start(f32[8,512]{1,0:T(8,128)S(1)} %fusion), channel_id=1, source_target_pairs={{0,9},{1,10},{2,11},{3,12},{4,13},{5,14},{6,15},{7,16},{8,17},{9,1... | collective-permute-start | bytes 49160
  1213.9 65.7 %collective-permute-start.7 = (f32[8,512]{1,0:T(8,128)S(1)}, f32[8,512]{1,0:T(8,128)}, u32[]{:S(2)}, u32[]{:S(2)}) collective-permute-start(f32[8,512]{1,0:T(8,128)S(1)} %fusion), channel_id=1, source_target_pairs={{0,8},{1,9},{2,10},{3,11},{4,12},{5,13},{6,14},{7,15},{8,16},{9,17... | collective-permute-start | bytes 49160
  1227.0 65.7 %collective-permute-start.6 = (f32[8,512]{1,0:T(8,128)S(1)}, f32[8,512]{1,0:T(8,128)}, u32[]{:S(2)}, u32[]{:S(2)}) collective-permute-start(f32[8,512]{1,0:T(8,128)S(1)} %fusion), channel_id=1, source_target_pairs={{0,7},{1,8},{2,9},{3,10},{4,11},{5,12},{6,13},{7,14},{8,15},{9,16}... | collective-permute-start | bytes 49160
  1240.2 65.7 %collective-permute-start.5 = (f32[8,512]{1,0:T(8,128)S(1)}, f32[8,512]{1,0:T(8,128)}, u32[]{:S(2)}, u32[]{:S(2)}) collective-permute-start(f32[8,512]{1,0:T(8,128)S(1)} %fusion), channel_id=1, source_target_pairs={{0,6},{1,7},{2,8},{3,9},{4,10},{5,11},{6,12},{7,13},{8,14},{9,15},... | collective-permute-start | bytes 49160
  1253.3 66.1 %collective-permute-start.4 = (f32[8,512]{1,0:T(8,128)S(1)}, f32[8,512]{1,0:T(8,128)}, u32[]{:S(2)}, u32[]{:S(2)}) collective-permute-start(f32[8,512]{1,0:T(8,128)S(1)} %fusion), channel_id=1, source_target_pairs={{0,5},{1,6},{2,7},{3,8},{4,9},{5,10},{6,11},{7,12},{8,13},{9,14},{... | collective-permute-start | bytes 49160
  1266.4 53.0 %collective-permute-start.3 = (f32[8,512]{1,0:T(8,128)S(1)}, f32[8,512]{1,0:T(8,128)}, u32[]{:S(2)}, u32[]{:S(2)}) collective-permute-start(f32[8,512]{1,0:T(8,128)S(1)} %fusion), channel_id=1, source_target_pairs={{0,4},{1,5},{2,6},{3,7},{4,8},{5,9},{6,10},{7,11},{8,12},{9,13},{1... | collective-permute-start | bytes 49160
  1279.6 39.8 %collective-permute-start.2 = (f32[8,512]{1,0:T(8,128)S(1)}, f32[8,512]{1,0:T(8,128)}, u32[]{:S(2)}, u32[]{:S(2)}) collective-permute-start(f32[8,512]{1,0:T(8,128)S(1)} %fusion), channel_id=1, source_target_pairs={{0,3},{1,4},{2,5},{3,6},{4,7},{5,8},{6,9},{7,10},{8,11},{9,12},{10... | collective-permute-start | bytes 49160
  1292.7 26.7 %collective-permute-start.1 = (f32[8,512]{1,0:T(8,128)S(1)}, f32[8,512]{1,0:T(8,128)}, u32[]{:S(2)}, u32[]{:S(2)}) collective-permute-start(f32[8,512]{1,0:T(8,128)S(1)} %fusion), channel_id=1, source_target_pairs={{0,2},{1,3},{2,4},{3,5},{4,6},{5,7},{6,8},{7,9},{8,10},{9,11},{10,... | collective-permute-start | bytes 49160
  1305.9 21.0 %collective-permute-start = (f32[8,512]{1,0:T(8,128)S(1)}, f32[8,512]{1,0:T(8,128)}, u32[]{:S(2)}, u32[]{:S(2)}) collective-permute-start(f32[8,512]{1,0:T(8,128)S(1)} %fusion), channel_id=1, source_target_pairs={{0,1},{1,2},{2,3},{3,4},{4,5},{5,6},{6,7},{7,8},{8,9},{9,10},{10,1... | collective-permute-start | bytes 49160
  (60 other events, 13735.5 us)
Sparse Core Ops, SparseCore 0:
  11.2 69.6 all-gather.1
  97.2 85.4 reduce-scatter.6
  189.5 282.0 all-reduce.6
where the time goes:
time: 1450 us; the launch traced here: 1430 us
  blocking collectives  647 us (45%)
  starting transfers between devices  483 us (33%)
  waiting for transfers between devices  152 us (10%)
  local copies, waits for them, and re-layouts  98.9 us (7%)
  matrix products  30.7 us (2%)
  between operations  16.4 us (1%)
    unnamed x1, blocking collectives  647 us
    unnamed x66, starting transfers between devices  483 us
    unnamed x121, local copies, waits for them, and re-layouts  98.9 us
    unnamed x69, waiting for transfers between devices  85.2 us
    all_gather x1, waiting for transfers between devices, body(): keyval = lax.all_gather(local_kv, 'seq', axis=0, tiled=True)  66.4 us
  transfers between devices with their start and end apart: 67, of which 3 were waited for; matrix products, arithmetic and copies ran while one was open for 53% of the time, Pallas kernels for 0%

commit v1 on v0

v1 whole, which is shorter than its diff:
```python
import functools

import jax
import jax.numpy as jnp
from jax import lax
from jax.experimental import pallas as pl
from jax.experimental.pallas import tpu as pltpu
from jax.sharding import PartitionSpec as P

EPS = 1e-06
HK = 128
HV = 192
HEADS = 4
KV = HK + HV
D = 1536
ROWS = 128
ALL = HEADS * ROWS
CHUNK = 512
LOG2E = 1.4426950408889634
SCALE = HK ** (-0.5)
F32 = jnp.float32
BF16 = jnp.bfloat16
NT = (((1,), (1,)), ((), ()))
NN = (((1,), (0,)), ((), ()))

COLS = (HEADS * HV, HEADS * HK, KV)


def mm(a, b, dims=NN):
    return lax.dot_general(a, b, dims, preferred_element_type=F32)


def make_slots():
    names = []
    names += [("agz", d) for d in (1, 2, 3)]
    names += [("agy", j, d) for j in (1, 3) for d in range(4)]
    names += [("agr", d) for d in range(4)]
    names += [("sib", k) for k in ("n", "c", "a", "q", "kv")]
    names += [("rs1", j, s) for j in (1, 3) for s in ("opp", "own")]
    names += [("rs2", j) for j in (1, 3)]
    names += [("rsz", d) for d in (1, 2, 3)]
    for w in range(3):
        names += [("wx1", w, h) for h in (0, 1)]
        names += [("wx2", w, h) for h in (0, 1)]
        names += [("wy", w, j) for j in (1, 2, 3)]
        names += [("wz", w, a, b) for a in (0, 1) for b in range(4) if a or b]
    return {name: i for i, name in enumerate(names)}


SLOT = make_slots()


def kernel(
    len_ref, tok_ref, cot_ref, gain_ref, wq_ref, wkv_ref, wo_ref,
    gtok_ref, gwq_ref, gwkv_ref, gwo_ref,
    kvt, vals, scores, probs, ub, qt, qts, dat, dats, normed, rscale, dn,
    t, r1a, r1b, fa, fb, r2a, r2b, zsend, rz,
    nall, call, n2, c2, a2, dq2, dkv2,
    p0, p1, p2, rx0, rx1, rx2, fx0, fx1, fx2, sx0, sx1, sx2,
    y0, y1, y2, ry0, ry1, ry2, ys0, ys1, ys2, z0, z1, z2, rz0, rz1, rz2,
    ssem, rsem,
):
    dp, seq = lax.axis_index("dp"), lax.axis_index("seq")
    x, zh, c = dp // 4, (dp // 2) % 2, dp % 2
    y, zl = seq // 4, seq % 4
    xs = (x, x + 1 - 2 * (x % 2), (x + 2) % 4, 3 - x)
    ys = (y, y + 1 - 2 * (y % 2), (y + 2) % 4, 3 - y)
    other = 1 - c

    def dev(x_=x, zh_=zh, c_=c, y_=y, zl_=zl):
        return (x_ * 4 + zh_ * 2 + c_, y_ * 4 + zl_)

    sent = []

    def send(name, src, dst, to):
        i = SLOT[name]
        copy = pltpu.make_async_remote_copy(
            src_ref=src, dst_ref=dst, send_sem=ssem.at[i], recv_sem=rsem.at[i],
            device_id=to, device_id_type=pl.DeviceIdType.MESH,
        )
        copy.start()
        sent.append(copy)
        return copy

    peers = [dev(c_=other), dev(x_=xs[1]), dev(x_=xs[3])]
    peers += [dev(y_=ys[j]) for j in (1, 2, 3)]
    peers += [
        dev(zh_=(zh + a) % 2, zl_=(zl + b) % 4) for a in (0, 1) for b in range(4) if a or b
    ]
    barrier = pltpu.get_barrier_semaphore()
    for peer in peers:
        pl.semaphore_signal(barrier, inc=1, device_id=peer, device_id_type=pl.DeviceIdType.MESH)

    xf = tok_ref[...].astype(F32)
    rs = lax.rsqrt(jnp.mean(xf * xf, axis=-1, keepdims=True) + EPS)
    rscale[...] = rs
    nf = xf * rs * gain_ref[...]
    nb = nf.astype(BF16)
    normed[...] = nb
    kv = mm(nb, wkv_ref[...])
    kvt[0, :, 0:ROWS] = kv.T.astype(BF16)
    pl.semaphore_wait(barrier, len(peers))

    agz, agy, agr = {}, {}, {}
    lane = [slice(ROWS * d, ROWS * (d + 1)) for d in range(4)]

    def to_y(d):
        for j in (1, 3):
            agy[j, d] = send(("agy", j, d), kvt.at[0, :, lane[d]], kvt.at[j, :, lane[d]], dev(y_=ys[j]))

    for d in (1, 3, 2):
        agz[d] = send(("agz", d), kvt.at[0, :, lane[0]], kvt.at[0, :, lane[d]], dev(zl_=(zl + 4 - d) % 4))
    to_y(0)

    q = mm(normed[...], wq_ref[...])
    for h in range(HEADS):
        qt[:, lane[h]] = q[:, lane[h]].T.astype(BF16)
    for d in (1, 3):
        agz[d].wait_recv()
        to_y(d)
    for h in range(HEADS):
        da = mm(wo_ref[HV * h : HV * (h + 1), :], cot_ref[...], NT)
        dat[:, lane[h]] = da.astype(BF16)
    agz[2].wait_recv()
    to_y(2)

    nall[...] = normed[...].T.reshape(4, 2, 2, 96, ROWS)
    sib = dev(c_=other)
    sib_n = send(("sib", "n"), nall.at[:, :, other], n2.at[:, :, :, ROWS : 2 * ROWS], sib)
    n2[:, :, :, 0:ROWS] = nall[:, :, c]
    call[...] = cot_ref[...].T.reshape(4, 2, 2, 96, ROWS)
    sib_c = send(("sib", "c"), call.at[:, :, other], c2.at[:, :, :, ROWS : 2 * ROWS], sib)
    c2[:, :, :, 0:ROWS] = call[:, :, c]

    length = len_ref[0]
    tops = [None]

    def score(j, d):
        first = (ys[j] * 4 + (zl + d) % 4) * ROWS
        blk = kvt[j, :, lane[d]]
        k = blk[0:HK, :].T
        vals[j, lane[d], :] = blk[HK:KV, :].T
        s = mm(k, qt[...]) * (SCALE * LOG2E)
        pos = first + lax.broadcasted_iota(jnp.int32, (ROWS, ALL), 0)
        s = jnp.where(pos < length, s, -1e30)
        scores[j, lane[d], :] = s
        part = jnp.max(s.reshape(ROWS // 8, 8, ALL), axis=0)
        tops[0] = part if tops[0] is None else jnp.maximum(tops[0], part)

    for d in range(4):
        score(0, d)
    relay = {}
    for d, j, to in ((0, 1, 3), (2, 3, 1), (1, 1, 3), (3, 3, 1)):
        agy[j, d].wait_recv()
        relay[d] = send(("agr", d), kvt.at[j, :, lane[d]], kvt.at[2, :, lane[d]], dev(y_=ys[to]))
        score(j, d)
    for j, d in ((1, 2), (1, 3), (3, 0), (3, 1)):
        agy[j, d].wait_recv()
        score(j, d)
    for d in (0, 2, 1, 3):
        relay[d].wait_recv()
        score(2, d)

    top = jnp.max(tops[0], axis=0, keepdims=True)
    total = jnp.zeros((8, ALL), F32)
    att = jnp.zeros((HV, ALL), F32)
    for j in range(4):
        for d in range(4):
            e = jnp.exp2(scores[j, lane[d], :] - top)
            total = total + jnp.sum(e.reshape(ROWS // 8, 8, ALL), axis=0)
            probs[j, lane[d], :] = e.astype(BF16)
        att = att + mm(kvt[j, HK:KV, :], probs[j])
    inv = 1.0 / jnp.sum(total, axis=0, keepdims=True)
    att_b = (att * inv).astype(BF16)
    da = dat[...].astype(F32)
    delta = jnp.sum(da * att_b.astype(F32), axis=0, keepdims=True)
    dats[...] = (da * inv).astype(BF16)
    qts[...] = (qt[...].astype(F32) * (inv * SCALE)).astype(BF16)
    for h in range(HEADS):
        a2[HV * h : HV * (h + 1), 0:ROWS] = att_b[:, lane[h]]
    mine, theirs = slice(0, ROWS), slice(ROWS, 2 * ROWS)
    sib_a = send(("sib", "a"), a2.at[:, mine], a2.at[:, theirs], sib)

    def backward(j, dq):
        for d in range(4):
            dpv = mm(vals[j, lane[d], :], dat[...])
            u = probs[j, lane[d], :].astype(F32) * (dpv - delta)
            ub[j, lane[d], :] = u.astype(BF16)
        dq = dq + mm(kvt[j, 0:HK, :], ub[j])
        t[j, 0:HK, :] = mm(qts[...], ub[j], NT).astype(BF16)
        t[j, HK:KV, :] = mm(dats[...], probs[j], NT).astype(BF16)
        return dq

    alpha, beta = slice(0, 256), slice(256, 512)
    to1, to3 = dev(y_=ys[1]), dev(y_=ys[3])
    rs1 = {}
    dq = backward(2, jnp.zeros((HK, ALL), F32))
    rs1[1, "opp"] = send(("rs1", 1, "opp"), t.at[2, :, alpha], r1a.at[1], to1)
    rs1[3, "opp"] = send(("rs1", 3, "opp"), t.at[2, :, beta], r1b.at[1], to3)
    dq = backward(1, dq)
    rs1[1, "own"] = send(("rs1", 1, "own"), t.at[1, :, alpha], r1a.at[0], to1)
    dq = backward(3, dq)
    rs1[3, "own"] = send(("rs1", 3, "own"), t.at[3, :, beta], r1b.at[0], to3)

    part, rx, fx, sx = (p0, p1, p2), (rx0, rx1, rx2), (fx0, fx1, fx2), (sx0, sx1, sx2)
    yb, ry, ysum = (y0, y1, y2), (ry0, ry1, ry2), (ys0, ys1, ys2)
    zb, rzb = (z0, z1, z2), (rz0, rz1, rz2)
    grads = (gwo_ref, gwq_ref, gwkv_ref)
    x1, x3 = dev(x_=xs[1]), dev(x_=xs[3])
    wx1, wx2, wy, wz = {}, {}, {}, {}

    def w_part(w, rows, right):
        for i in (2, 1, 3, 0):
            left = rows[xs[i]].reshape(192, 2 * ROWS)
            part[w][i] = mm(left, right[...], NT).reshape(2, 96, COLS[w]).astype(BF16)
            if i == 1:
                wx1[w, 0] = send(("wx1", w, 0), part[w].at[1:3, 0], rx[w].at[0], x1)
            if i == 3:
                wx1[w, 1] = send(("wx1", w, 1), part[w].at[2:4, 1], rx[w].at[1], x3)

    def w_x2(w):
        wx1[w, 0].wait_recv()
        fx[w][0] = (part[w][3, 0].astype(F32) + rx[w][0, 1].astype(F32)).astype(BF16)
        wx2[w, 0] = send(("wx2", w, 0), fx[w].at[0], sx[w].at[0], x3)
        wx1[w, 1].wait_recv()
        fx[w][1] = (part[w][1, 1].astype(F32) + rx[w][1, 0].astype(F32)).astype(BF16)
        wx2[w, 1] = send(("wx2", w, 1), fx[w].at[1], sx[w].at[1], x1)

    def w_y(w):
        sums = []
        for h in (0, 1):
            wx2[w, h].wait_recv()
            sums.append(
                part[w][0, h].astype(F32) + rx[w][h, h].astype(F32) + sx[w][h].astype(F32)
            )
        for k in range(4):
            rows = slice(24 * k, 24 * (k + 1))
            yb[w][k] = jnp.concatenate([sums[0][rows], sums[1][rows]], axis=0).astype(BF16)
        for j in (2, 1, 3):
            wy[w, j] = send(("wy", w, j), yb[w].at[ys[j]], ry[w].at[j - 1], dev(y_=ys[j]))

    def w_z(w):
        total = yb[w][y].astype(F32)
        for j in (1, 3, 2):
            wy[w, j].wait_recv()
            total = total + ry[w][j - 1].astype(F32)
        ysum[w][...] = total
        zb[w][...] = jnp.zeros_like(zb[w])
        for k in range(8):
            zb[w][k, 0:6, :] = ysum[w][6 * k : 6 * (k + 1), :]
        for a, b in ((1, 0), (1, 1), (1, 3), (1, 2), (0, 2), (0, 1), (0, 3)):
            zh_, zl_ = (zh + a) % 2, (zl + b) % 4
            wz[w, a, b] = send(
                ("wz", w, a, b), zb[w].at[zh_ * 4 + zl_], rzb[w].at[a * 4 + b - 1], dev(zh_=zh_, zl_=zl_)
            )

    def w_end(w):
        total = zb[w][zh * 4 + zl]
        for a, b in ((0, 1), (0, 3), (0, 2), (1, 0), (1, 1), (1, 3), (1, 2)):
            wz[w, a, b].wait_recv()
            total = total + rzb[w][a * 4 + b - 1]
        grads[w][...] = total[0:6, :]

    sib_c.wait_recv()
    sib_a.wait_recv()
    w_part(0, c2, a2)

    dq = backward(0, dq)
    dq_b = (dq * (inv * SCALE)).astype(BF16)
    for h in range(HEADS):
        dq2[HK * h : HK * (h + 1), mine] = dq_b[:, lane[h]]
    sib_q = send(("sib", "q"), dq2.at[:, mine], dq2.at[:, theirs], sib)

    rs1[1, "opp"].wait_recv()
    fa[...] = (t[3, :, alpha].astype(F32) + r1a[1].astype(F32)).astype(BF16)
    rs2a = send(("rs2", 3), fa, r2a, to3)
    rs1[3, "opp"].wait_recv()
    fb[...] = (t[1, :, beta].astype(F32) + r1b[1].astype(F32)).astype(BF16)
    rs2b = send(("rs2", 1), fb, r2b, to1)

    sib_n.wait_recv()
    sib_q.wait_recv()
    w_part(1, n2, dq2)
    w_x2(0)

    rs1[1, "own"].wait_recv()
    rs2a.wait_recv()
    sum_a = t[0, :, alpha].astype(F32) + r1a[0].astype(F32) + r2a[...].astype(F32)
    zsend[:, alpha] = sum_a.astype(BF16)
    rsz = {}
    rsz[1] = send(("rsz", 1), zsend.at[:, lane[1]], rz.at[0], dev(zl_=(zl + 1) % 4))
    rs1[3, "own"].wait_recv()
    rs2b.wait_recv()
    sum_b = t[0, :, beta].astype(F32) + r1b[0].astype(F32) + r2b[...].astype(F32)
    zsend[:, beta] = sum_b.astype(BF16)
    for d in (2, 3):
        rsz[d] = send(("rsz", d), zsend.at[:, lane[d]], rz.at[d - 1], dev(zl_=(zl + d) % 4))

    w_x2(1)
    dqn = jnp.concatenate([dq2[HK * h : HK * (h + 1), mine].T for h in range(HEADS)], axis=1)
    dn[...] = mm(dqn, wq_ref[...], NT)
    w_y(0)

    dkv = zsend[:, lane[0]].astype(F32)
    for d in (1, 2, 3):
        rsz[d].wait_recv()
        dkv = dkv + rz[d - 1].astype(F32)
    dkv_b = dkv.astype(BF16)
    dkv2[:, mine] = dkv_b
    sib_kv = send(("sib", "kv"), dkv2.at[:, mine], dkv2.at[:, theirs], sib)
    dkvn = jnp.concatenate([dkv_b[0:HK].T, dkv_b[HK:KV].T], axis=1)
    sib_kv.wait_recv()
    w_part(2, n2, dkv2)

    w_y(1)
    d_normed = dn[...] + mm(dkvn, wkv_ref[...], NT)
    w_x2(2)
    w_z(0)
    xf = tok_ref[...].astype(F32)
    rs = rscale[...]
    gd = gain_ref[...] * d_normed
    inner = jnp.mean(xf * gd, axis=-1, keepdims=True)
    out = cot_ref[...].astype(F32) + rs * gd - xf * (rs * rs * rs * inner)
    gtok_ref[...] = out.astype(BF16)
    w_y(2)
    w_z(1)
    w_z(2)
    for w in range(3):
        w_end(w)
    for copy in sent:
        copy.wait_send()


def body(tokens, lengths, cotangent, gain, w_q, w_kv, w_o):
    vmem = pl.BlockSpec(memory_space=pltpu.VMEM)
    smem = pl.BlockSpec(memory_space=pltpu.SMEM)

    def per_weight(shape, kind):
        return [pltpu.VMEM(shape(n), kind) for n in COLS]

    scratch = [
        pltpu.VMEM((4, KV, CHUNK), BF16),
        pltpu.VMEM((4, CHUNK, HV), BF16),
        pltpu.VMEM((4, CHUNK, ALL), F32),
        pltpu.VMEM((4, CHUNK, ALL), BF16),
        pltpu.VMEM((4, CHUNK, ALL), BF16),
        pltpu.VMEM((HK, ALL), BF16),
        pltpu.VMEM((HK, ALL), BF16),
        pltpu.VMEM((HV, ALL), BF16),
        pltpu.VMEM((HV, ALL), BF16),
        pltpu.VMEM((ROWS, D), BF16),
        pltpu.VMEM((ROWS, 1), F32),
        pltpu.VMEM((ROWS, D), F32),
        pltpu.VMEM((4, KV, CHUNK), BF16),
        pltpu.VMEM((2, KV, 256), BF16),
        pltpu.VMEM((2, KV, 256), BF16),
        pltpu.VMEM((KV, 256), BF16),
        pltpu.VMEM((KV, 256), BF16),
        pltpu.VMEM((KV, 256), BF16),
        pltpu.VMEM((KV, 256), BF16),
        pltpu.VMEM((KV, CHUNK), BF16),
        pltpu.VMEM((3, KV, ROWS), BF16),
        pltpu.VMEM((4, 2, 2, 96, ROWS), BF16),
        pltpu.VMEM((4, 2, 2, 96, ROWS), BF16),
        pltpu.VMEM((4, 2, 96, 2 * ROWS), BF16),
        pltpu.VMEM((4, 2, 96, 2 * ROWS), BF16),
        pltpu.VMEM((COLS[0], 2 * ROWS), BF16),
        pltpu.VMEM((COLS[1], 2 * ROWS), BF16),
        pltpu.VMEM((COLS[2], 2 * ROWS), BF16),
    ]
    scratch += per_weight(lambda n: (4, 2, 96, n), BF16)
    scratch += per_weight(lambda n: (2, 2, 96, n), BF16)
    scratch += per_weight(lambda n: (2, 96, n), BF16)
    scratch += per_weight(lambda n: (2, 96, n), BF16)
    scratch += per_weight(lambda n: (4, 48, n), BF16)
    scratch += per_weight(lambda n: (3, 48, n), BF16)
    scratch += per_weight(lambda n: (48, n), F32)
    scratch += per_weight(lambda n: (8, 8, n), F32)
    scratch += per_weight(lambda n: (7, 8, n), F32)
    scratch += [pltpu.SemaphoreType.DMA((len(SLOT),)), pltpu.SemaphoreType.DMA((len(SLOT),))]
    grad_x, grad_wq, grad_wkv, grad_wo_t = pl.pallas_call(
        kernel,
        out_shape=(
            jax.ShapeDtypeStruct((ROWS, D), BF16),
            jax.ShapeDtypeStruct((6, COLS[1]), F32),
            jax.ShapeDtypeStruct((6, COLS[2]), F32),
            jax.ShapeDtypeStruct((6, COLS[0]), F32),
        ),
        in_specs=[smem] + [vmem] * 6,
        out_specs=(vmem,) * 4,
        scratch_shapes=scratch,
        compiler_params=pltpu.CompilerParams(
            collective_id=0, has_side_effects=True, vmem_limit_bytes=56 * 1024 * 1024
        ),
    )(lengths, tokens[0], cotangent[0], gain[None, :], w_q, w_kv, w_o)
    return grad_x[None], grad_wq, grad_wkv, grad_wo_t


def solution(mesh):
    return jax.shard_map(
        body,
        mesh=mesh,
        in_specs=(P("dp", "seq", None), P("dp"), P("dp", "seq", None), P(), P(), P(), P()),
        out_specs=(
            P("dp", "seq", None),
            P(("dp", "seq"), None),
            P(("dp", "seq"), None),
            P(("dp", "seq"), None),
        ),
        check_vma=False,
    )
```

time: 1450 us -> 82.7 us (0.06); the launches traced: 1430 us -> 82.3 us
  blocking collectives: 647 us -> 0 us
  starting transfers between devices: 483 us -> 0 us
  waiting for transfers between devices: 152 us -> 0 us
  local copies, waits for them, and re-layouts: 98.9 us -> 9.38 us
  Pallas kernels: 0 us -> 71.6 us
  matrix products: 30.7 us -> 0 us
  between operations: 16.4 us -> 1.29 us
    unnamed x1 -> x0, blocking collectives: 647 us -> none
    unnamed x66 -> x0, starting transfers between devices: 483 us -> none
    unnamed x121 -> x5, local copies, waits for them, and re-layouts: 98.9 us -> 8.08 us
    unnamed x69 -> x0, waiting for transfers between devices: 85.2 us -> none
    pallas_call x0 -> x1, Pallas kernels: none -> 71.6 us  [body(): pl.pallas_call(kernel, out_shape=(jax.ShapeDtypeStruct((ROWS, D), BF16),...]
    all_gather x1 -> x0, waiting for transfers between devices: 66.4 us -> none  [body(): keyval = lax.all_gather(local_kv, 'seq', axis=0, tiled=True)]
    dot_general x32 -> x0, matrix products: 30.7 us -> none  [the longest x4 4.85 us: body(): jnp.dot(d_score, keys, preferred_element_type=jnp.float32)]
  transfers between devices with their start and end apart: 67 -> 0, of which waited for: 3 -> 0; matrix products, arithmetic and copies ran while one was open for 53% -> 0% of each run, Pallas kernels for 0% -> 0%
where the time goes in v1:
time: 82.7 us; the launch traced here: 82.3 us
  Pallas kernels  71.6 us (87%)
  local copies, waits for them, and re-layouts  9.38 us (11%)
  between operations  1.29 us (2%)
    pallas_call x1, Pallas kernels, body(): pl.pallas_call(kernel, out_shape=(jax.ShapeDtypeStruct((ROWS, D), BF16),...  71.6 us
    unnamed x5, local copies, waits for them, and re-layouts  8.08 us

profile of v1, /device:TPU:1, one launch (start us, length us, event | category | flops | bytes accessed | tf_op | source)
XLA Modules:
  0.0 82.3 jit_solution(13041042892174513317)
XLA Ops:
  1.3 1.3 %broadcast_in_dim.6.gain_ref = f32[1,1536]{1,0:T(1,128)} reshape(f32[1536]{0:T(1024)} %param.10) | data formatting | bytes 12288 | tf_op jit(solution)/shard_map/broadcast_in_dim | solution.py:395
  2.6 2.3 %copy.11.wkv_ref = bf16[1536,320]{1,0:T(8,128)(2,1)} copy(bf16[1536,320]{0,1:T(8,128)(2,1)} %param.12) | data formatting | bytes 1966080 | tf_op args[5]
  4.9 71.6 %shard_map.102 = (bf16[128,1536]{1,0:T(8,128)(2,1)}, f32[6,512]{1,0:T(8,128)}, f32[6,320]{1,0:T(8,128)}, f32[6,768]{1,0:T(8,128)}) custom-call(s32[1]{0:T(128)S(6)} %copy.16.len_ref, bf16[128,1536]{1,0:T(8,128)(2,1)} %bitcast.3, bf16[128,1536]{1,0:T(8,128)(2,1)} %bitcast.4, f32[1,1536]{1,0:T(1,128)} %broadcast_in_dim.6.gain_ref, bf16[1536,512]{1,0:T(8,128)(2,1)} %wq_ref.1, ...), custom_call_target="tpu_custom_call" | custom-call | tf_op jit(solution)/shard_map/pallas_call | solution.py:381
  76.6 1.8 %copy.17 = bf16[1,128,1536]{2,1,0:T(8,128)(2,1)} copy(bf16[1,128,1536]{2,1,0:T(8,128)(2,1)} %bitcast.5) | data formatting | bytes 786432
  78.3 1.3 %copy.18 = f32[6,512]{1,0:T(8,128)} copy(f32[6,512]{1,0:T(8,128)} %get-tuple-element.17) | data formatting | bytes 24576
  79.6 1.3 %copy.19 = f32[6,320]{1,0:T(8,128)} copy(f32[6,320]{1,0:T(8,128)} %get-tuple-element.18) | data formatting | bytes 15360
  81.0 1.3 %copy.20 = f32[6,768]{1,0:T(8,128)} copy(f32[6,768]{1,0:T(8,128)} %get-tuple-element.19) | data formatting | bytes 36864

commit v2 on v1

--- a/solution.py
+++ b/solution.py
@@ -36,13 +36,15 @@
     names += [("agy", j, d) for j in (1, 3) for d in range(4)]
     names += [("agr", d) for d in range(4)]
     names += [("sib", k) for k in ("n", "c", "a", "q", "kv")]
-    names += [("rs1", j, s) for j in (1, 3) for s in ("opp", "own")]
-    names += [("rs2", j) for j in (1, 3)]
+    names += [("rs1", d, k) for d in range(4) for k in (0, 1)]
+    names += [("rs2", d) for d in range(4)]
     names += [("rsz", d) for d in (1, 2, 3)]
-    for w in range(3):
+    for w in range(2):
         names += [("wx1", w, h) for h in (0, 1)]
         names += [("wx2", w, h) for h in (0, 1)]
         names += [("wy", w, j) for j in (1, 2, 3)]
+    names += [("wxy", i, j) for i in range(4) for j in range(4) if i or j]
+    for w in range(3):
         names += [("wz", w, a, b) for a in (0, 1) for b in range(4) if a or b]
     return {name: i for i, name in enumerate(names)}
 
@@ -51,14 +53,16 @@
 
 
 def kernel(
+    len_hbm, tok_hbm, cot_hbm, gain_hbm, wq_hbm, wkv_hbm, wo_hbm,
+    gtok_hbm, gwq_hbm, gwkv_hbm, gwo_hbm,
     len_ref, tok_ref, cot_ref, gain_ref, wq_ref, wkv_ref, wo_ref,
     gtok_ref, gwq_ref, gwkv_ref, gwo_ref,
     kvt, vals, scores, probs, ub, qt, qts, dat, dats, normed, rscale, dn,
-    t, r1a, r1b, fa, fb, r2a, r2b, zsend, rz,
+    t, r1, f, r2, zsend, rz,
     nall, call, n2, c2, a2, dq2, dkv2,
-    p0, p1, p2, rx0, rx1, rx2, fx0, fx1, fx2, sx0, sx1, sx2,
-    y0, y1, y2, ry0, ry1, ry2, ys0, ys1, ys2, z0, z1, z2, rz0, rz1, rz2,
-    ssem, rsem,
+    p0, p1, rx0, rx1, fx0, fx1, sx0, sx1, y0, y1, ry0, ry1,
+    pk, rk, ys0, ys1, ys2, z0, z1, z2, rz0, rz1, rz2,
+    ssem, rsem, isem, osem,
 ):
     dp, seq = lax.axis_index("dp"), lax.axis_index("seq")
     x, zh, c = dp // 4, (dp // 2) % 2, dp % 2
@@ -82,23 +86,39 @@
         sent.append(copy)
         return copy
 
-    peers = [dev(c_=other), dev(x_=xs[1]), dev(x_=xs[3])]
-    peers += [dev(y_=ys[j]) for j in (1, 2, 3)]
+    peers = [dev(c_=other)]
+    peers += [dev(x_=xs[i], y_=ys[j]) for i in range(4) for j in range(4) if i or j]
     peers += [
         dev(zh_=(zh + a) % 2, zl_=(zl + b) % 4) for a in (0, 1) for b in range(4) if a or b
     ]
+    loads = {}
+
+    def load(i, name, src, dst):
+        loads[name] = pltpu.make_async_copy(src, dst, isem.at[i])
+        loads[name].start()
+
+    load(0, "tok", tok_hbm, tok_ref)
+    load(1, "gain", gain_hbm, gain_ref)
+    load(2, "wkv", wkv_hbm, wkv_ref)
     barrier = pltpu.get_barrier_semaphore()
     for peer in peers:
         pl.semaphore_signal(barrier, inc=1, device_id=peer, device_id_type=pl.DeviceIdType.MESH)
 
+    loads["tok"].wait()
+    loads["gain"].wait()
+    load(3, "wq", wq_hbm, wq_ref)
+    load(4, "cot", cot_hbm, cot_ref)
+    load(5, "wo", wo_hbm, wo_ref)
+    load(6, "len", len_hbm, len_ref)
+    gain = gain_ref[...].reshape(1, D)
     xf = tok_ref[...].astype(F32)
     rs = lax.rsqrt(jnp.mean(xf * xf, axis=-1, keepdims=True) + EPS)
     rscale[...] = rs
-    nf = xf * rs * gain_ref[...]
+    nf = xf * rs * gain
     nb = nf.astype(BF16)
     normed[...] = nb
-    kv = mm(nb, wkv_ref[...])
-    kvt[0, :, 0:ROWS] = kv.T.astype(BF16)
+    loads["wkv"].wait()
+    kvt[0, :, 0:ROWS] = mm(wkv_ref[...], nb, NT).astype(BF16)
     pl.semaphore_wait(barrier, len(peers))
 
     agz, agy, agr = {}, {}, {}
@@ -108,30 +128,41 @@
         for j in (1, 3):
             agy[j, d] = send(("agy", j, d), kvt.at[0, :, lane[d]], kvt.at[j, :, lane[d]], dev(y_=ys[j]))
 
-    for d in (1, 3, 2):
+    def to_z(d):
         agz[d] = send(("agz", d), kvt.at[0, :, lane[0]], kvt.at[0, :, lane[d]], dev(zl_=(zl + 4 - d) % 4))
+
+    def relay_y(d):
+        j, to = ((1, 3), (1, 3), (3, 1), (3, 1))[d]
+        agy[j, d].wait_recv()
+        agr[d] = send(("agr", d), kvt.at[j, :, lane[d]], kvt.at[2, :, lane[d]], dev(y_=ys[to]))
+
+    def wait_z(d):
+        agz[d].wait_recv()
+        to_y(d)
+
+    to_z(1)
+    to_z(3)
     to_y(0)
-
+    to_z(2)
+    loads["wq"].wait()
     q = mm(normed[...], wq_ref[...])
     for h in range(HEADS):
         qt[:, lane[h]] = q[:, lane[h]].T.astype(BF16)
-    for d in (1, 3):
-        agz[d].wait_recv()
-        to_y(d)
+    relay_y(0)
+    loads["cot"].wait()
+    loads["wo"].wait()
     for h in range(HEADS):
         da = mm(wo_ref[HV * h : HV * (h + 1), :], cot_ref[...], NT)
         dat[:, lane[h]] = da.astype(BF16)
-    agz[2].wait_recv()
-    to_y(2)
-
+    wait_z(1)
+    wait_z(3)
     nall[...] = normed[...].T.reshape(4, 2, 2, 96, ROWS)
+    wait_z(2)
     sib = dev(c_=other)
     sib_n = send(("sib", "n"), nall.at[:, :, other], n2.at[:, :, :, ROWS : 2 * ROWS], sib)
     n2[:, :, :, 0:ROWS] = nall[:, :, c]
-    call[...] = cot_ref[...].T.reshape(4, 2, 2, 96, ROWS)
-    sib_c = send(("sib", "c"), call.at[:, :, other], c2.at[:, :, :, ROWS : 2 * ROWS], sib)
-    c2[:, :, :, 0:ROWS] = call[:, :, c]
-
+
+    loads["len"].wait()
     length = len_ref[0]
     tops = [None]
 
@@ -147,18 +178,23 @@
         part = jnp.max(s.reshape(ROWS // 8, 8, ALL), axis=0)
         tops[0] = part if tops[0] is None else jnp.maximum(tops[0], part)
 
-    for d in range(4):
-        score(0, d)
-    relay = {}
-    for d, j, to in ((0, 1, 3), (2, 3, 1), (1, 1, 3), (3, 3, 1)):
-        agy[j, d].wait_recv()
-        relay[d] = send(("agr", d), kvt.at[j, :, lane[d]], kvt.at[2, :, lane[d]], dev(y_=ys[to]))
+    score(0, 0)
+    score(0, 1)
+    relay_y(1)
+    score(0, 3)
+    score(0, 2)
+    relay_y(3)
+    relay_y(2)
+    for d, j in ((0, 1), (1, 1), (2, 3), (3, 3)):
         score(j, d)
-    for j, d in ((1, 2), (1, 3), (3, 0), (3, 1)):
+    call[...] = cot_ref[...].T.reshape(4, 2, 2, 96, ROWS)
+    sib_c = send(("sib", "c"), call.at[:, :, other], c2.at[:, :, :, ROWS : 2 * ROWS], sib)
+    c2[:, :, :, 0:ROWS] = call[:, :, c]
+    for j, d in ((3, 0), (3, 1), (1, 3), (1, 2)):
         agy[j, d].wait_recv()
         score(j, d)
-    for d in (0, 2, 1, 3):
-        relay[d].wait_recv()
+    for d in (0, 1, 3, 2):
+        agr[d].wait_recv()
         score(2, d)
 
     top = jnp.max(tops[0], axis=0, keepdims=True)
@@ -191,21 +227,32 @@
         t[j, HK:KV, :] = mm(dats[...], probs[j], NT).astype(BF16)
         return dq
 
-    alpha, beta = slice(0, 256), slice(256, 512)
-    to1, to3 = dev(y_=ys[1]), dev(y_=ys[3])
-    rs1 = {}
-    dq = backward(2, jnp.zeros((HK, ALL), F32))
-    rs1[1, "opp"] = send(("rs1", 1, "opp"), t.at[2, :, alpha], r1a.at[1], to1)
-    rs1[3, "opp"] = send(("rs1", 3, "opp"), t.at[2, :, beta], r1b.at[1], to3)
-    dq = backward(1, dq)
-    rs1[1, "own"] = send(("rs1", 1, "own"), t.at[1, :, alpha], r1a.at[0], to1)
-    dq = backward(3, dq)
-    rs1[3, "own"] = send(("rs1", 3, "own"), t.at[3, :, beta], r1b.at[0], to3)
-
-    part, rx, fx, sx = (p0, p1, p2), (rx0, rx1, rx2), (fx0, fx1, fx2), (sx0, sx1, sx2)
-    yb, ry, ysum = (y0, y1, y2), (ry0, ry1, ry2), (ys0, ys1, ys2)
+    rs1, rs2, rsz = {}, {}, {}
+    hop1, hop2 = (1, 1, 3, 3), (3, 3, 1, 1)
+
+    def rs_opp(d):
+        rs1[d, 1] = send(("rs1", d, 1), t.at[2, :, lane[d]], r1.at[d, 1], dev(y_=ys[hop1[d]]))
+
+    def rs_own(d):
+        rs1[d, 0] = send(("rs1", d, 0), t.at[hop1[d], :, lane[d]], r1.at[d, 0], dev(y_=ys[hop1[d]]))
+
+    def rs_fwd(d):
+        rs1[d, 1].wait_recv()
+        f[d] = (t[hop2[d], :, lane[d]].astype(F32) + r1[d, 1].astype(F32)).astype(BF16)
+        rs2[d] = send(("rs2", d), f.at[d], r2.at[d], dev(y_=ys[hop2[d]]))
+
+    def rs_sum(d):
+        rs1[d, 0].wait_recv()
+        rs2[d].wait_recv()
+        total = t[0, :, lane[d]].astype(F32) + r1[d, 0].astype(F32) + r2[d].astype(F32)
+        zsend[d] = total.astype(BF16)
+        if d:
+            rsz[d] = send(("rsz", d), zsend.at[d], rz.at[d - 1], dev(zl_=(zl + d) % 4))
+
+    part, rx, fx, sx = (p0, p1), (rx0, rx1), (fx0, fx1), (sx0, sx1)
+    yb, ry, ysum = (y0, y1), (ry0, ry1), (ys0, ys1, ys2)
     zb, rzb = (z0, z1, z2), (rz0, rz1, rz2)
-    grads = (gwo_ref, gwq_ref, gwkv_ref)
+    grads, grads_hbm = (gwo_ref, gwq_ref, gwkv_ref), (gwo_hbm, gwq_hbm, gwkv_hbm)
     x1, x3 = dev(x_=xs[1]), dev(x_=xs[3])
     wx1, wx2, wy, wz = {}, {}, {}, {}
 
@@ -239,11 +286,34 @@
         for j in (2, 1, 3):
             wy[w, j] = send(("wy", w, j), yb[w].at[ys[j]], ry[w].at[j - 1], dev(y_=ys[j]))
 
+    wxy = {}
+
+    def kv_part():
+        for i in (2, 1, 3, 0):
+            left = n2[xs[i]].reshape(192, 2 * ROWS)
+            rows = mm(left, dkv2[...], NT)
+            for k in range(4):
+                piece = [rows[96 * h + 24 * k : 96 * h + 24 * (k + 1)] for h in (0, 1)]
+                pk[i, k] = jnp.concatenate(piece, axis=0).astype(BF16)
+            for j in (2, 1, 3, 0):
+                if i or j:
+                    wxy[i, j] = send(
+                        ("wxy", i, j), pk.at[i, ys[j]], rk.at[4 * i + j], dev(x_=xs[i], y_=ys[j])
+                    )
+
     def w_z(w):
-        total = yb[w][y].astype(F32)
-        for j in (1, 3, 2):
-            wy[w, j].wait_recv()
-            total = total + ry[w][j - 1].astype(F32)
+        if w == 2:
+            total = pk[0, y].astype(F32)
+            for i in (0, 1, 3, 2):
+                for j in (0, 1, 3, 2):
+                    if i or j:
+                        wxy[i, j].wait_recv()
+                        total = total + rk[4 * i + j].astype(F32)
+        else:
+            total = yb[w][y].astype(F32)
+            for j in (1, 3, 2):
+                wy[w, j].wait_recv()
+                total = total + ry[w][j - 1].astype(F32)
         ysum[w][...] = total
         zb[w][...] = jnp.zeros_like(zb[w])
         for k in range(8):
@@ -261,47 +331,40 @@
             total = total + rzb[w][a * 4 + b - 1]
         grads[w][...] = total[0:6, :]
 
+    dq = backward(2, jnp.zeros((HK, ALL), F32))
+    for d in (1, 2, 0, 3):
+        rs_opp(d)
     sib_c.wait_recv()
     sib_a.wait_recv()
     w_part(0, c2, a2)
-
+    dq = backward(1, dq)
+    rs_own(1)
+    dq = backward(3, dq)
+    rs_own(2)
+    rs_fwd(1)
+    rs_fwd(2)
+    rs_own(0)
+    rs_own(3)
     dq = backward(0, dq)
     dq_b = (dq * (inv * SCALE)).astype(BF16)
     for h in range(HEADS):
         dq2[HK * h : HK * (h + 1), mine] = dq_b[:, lane[h]]
     sib_q = send(("sib", "q"), dq2.at[:, mine], dq2.at[:, theirs], sib)
-
-    rs1[1, "opp"].wait_recv()
-    fa[...] = (t[3, :, alpha].astype(F32) + r1a[1].astype(F32)).astype(BF16)
-    rs2a = send(("rs2", 3), fa, r2a, to3)
-    rs1[3, "opp"].wait_recv()
-    fb[...] = (t[1, :, beta].astype(F32) + r1b[1].astype(F32)).astype(BF16)
-    rs2b = send(("rs2", 1), fb, r2b, to1)
-
+    rs_fwd(0)
+    rs_fwd(3)
     sib_n.wait_recv()
     sib_q.wait_recv()
     w_part(1, n2, dq2)
+    rs_sum(1)
+    rs_sum(2)
     w_x2(0)
-
-    rs1[1, "own"].wait_recv()
-    rs2a.wait_recv()
-    sum_a = t[0, :, alpha].astype(F32) + r1a[0].astype(F32) + r2a[...].astype(F32)
-    zsend[:, alpha] = sum_a.astype(BF16)
-    rsz = {}
-    rsz[1] = send(("rsz", 1), zsend.at[:, lane[1]], rz.at[0], dev(zl_=(zl + 1) % 4))
-    rs1[3, "own"].wait_recv()
-    rs2b.wait_recv()
-    sum_b = t[0, :, beta].astype(F32) + r1b[0].astype(F32) + r2b[...].astype(F32)
-    zsend[:, beta] = sum_b.astype(BF16)
-    for d in (2, 3):
-        rsz[d] = send(("rsz", d), zsend.at[:, lane[d]], rz.at[d - 1], dev(zl_=(zl + d) % 4))
-
+    rs_sum(3)
+    rs_sum(0)
     w_x2(1)
     dqn = jnp.concatenate([dq2[HK * h : HK * (h + 1), mine].T for h in range(HEADS)], axis=1)
     dn[...] = mm(dqn, wq_ref[...], NT)
     w_y(0)
-
-    dkv = zsend[:, lane[0]].astype(F32)
+    dkv = zsend[0].astype(F32)
     for d in (1, 2, 3):
         rsz[d].wait_recv()
         dkv = dkv + rz[d - 1].astype(F32)
@@ -309,36 +372,62 @@
     dkv2[:, mine] = dkv_b
     sib_kv = send(("sib", "kv"), dkv2.at[:, mine], dkv2.at[:, theirs], sib)
     dkvn = jnp.concatenate([dkv_b[0:HK].T, dkv_b[HK:KV].T], axis=1)
+    dn[...] += mm(dkvn, wkv_ref[...])
     sib_kv.wait_recv()
-    w_part(2, n2, dkv2)
-
+    kv_part()
     w_y(1)
-    d_normed = dn[...] + mm(dkvn, wkv_ref[...], NT)
-    w_x2(2)
-    w_z(0)
     xf = tok_ref[...].astype(F32)
     rs = rscale[...]
-    gd = gain_ref[...] * d_normed
+    gd = gain_ref[...].reshape(1, D) * dn[...]
     inner = jnp.mean(xf * gd, axis=-1, keepdims=True)
     out = cot_ref[...].astype(F32) + rs * gd - xf * (rs * rs * rs * inner)
     gtok_ref[...] = out.astype(BF16)
-    w_y(2)
+    stores = [pltpu.make_async_copy(gtok_ref, gtok_hbm, osem.at[3])]
+    stores[0].start()
+    w_z(0)
     w_z(1)
     w_z(2)
     for w in range(3):
         w_end(w)
+        stores.append(pltpu.make_async_copy(grads[w], grads_hbm[w], osem.at[w]))
+        stores[-1].start()
     for copy in sent:
         copy.wait_send()
+    for copy in stores:
+        copy.wait()
+
+
+def hand_on(*refs):
+    come, go = refs[12], refs[13]
+    first = [pltpu.make_async_copy(refs[i], refs[8 + i], come.at[i]) for i in range(4)]
+    second = [pltpu.make_async_copy(refs[8 + i], refs[4 + i], go.at[i]) for i in range(4)]
+    for copy in first:
+        copy.start()
+    for i in range(4):
+        first[i].wait()
+        second[i].start()
+    for copy in second:
+        copy.wait()
 
 
 def body(tokens, lengths, cotangent, gain, w_q, w_kv, w_o):
-    vmem = pl.BlockSpec(memory_space=pltpu.VMEM)
-    smem = pl.BlockSpec(memory_space=pltpu.SMEM)
+    hbm = pl.BlockSpec(memory_space=pltpu.HBM)
 
     def per_weight(shape, kind):
         return [pltpu.VMEM(shape(n), kind) for n in COLS]
 
     scratch = [
+        pltpu.SMEM((1,), jnp.int32),
+        pltpu.VMEM((ROWS, D), BF16),
+        pltpu.VMEM((ROWS, D), BF16),
+        pltpu.VMEM((D,), F32),
+        pltpu.VMEM((D, COLS[1]), BF16),
+        pltpu.VMEM((KV, D), BF16),
+        pltpu.VMEM((HEADS * HV, D), BF16),
+        pltpu.VMEM((ROWS, D), BF16),
+        pltpu.VMEM((6, COLS[1]), F32),
+        pltpu.VMEM((6, COLS[2]), F32),
+        pltpu.VMEM((6, COLS[0]), F32),
         pltpu.VMEM((4, KV, CHUNK), BF16),
         pltpu.VMEM((4, CHUNK, HV), BF16),
         pltpu.VMEM((4, CHUNK, ALL), F32),
@@ -352,13 +441,10 @@
         pltpu.VMEM((ROWS, 1), F32),
         pltpu.VMEM((ROWS, D), F32),
         pltpu.VMEM((4, KV, CHUNK), BF16),
-        pltpu.VMEM((2, KV, 256), BF16),
-        pltpu.VMEM((2, KV, 256), BF16),
-        pltpu.VMEM((KV, 256), BF16),
-        pltpu.VMEM((KV, 256), BF16),
-        pltpu.VMEM((KV, 256), BF16),
-        pltpu.VMEM((KV, 256), BF16),
-        pltpu.VMEM((KV, CHUNK), BF16),
+        pltpu.VMEM((4, 2, KV, ROWS), BF16),
+        pltpu.VMEM((4, KV, ROWS), BF16),
+        pltpu.VMEM((4, KV, ROWS), BF16),
+        pltpu.VMEM((4, KV, ROWS), BF16),
         pltpu.VMEM((3, KV, ROWS), BF16),
         pltpu.VMEM((4, 2, 2, 96, ROWS), BF16),
         pltpu.VMEM((4, 2, 2, 96, ROWS), BF16),
@@ -368,31 +454,43 @@
         pltpu.VMEM((COLS[1], 2 * ROWS), BF16),
         pltpu.VMEM((COLS[2], 2 * ROWS), BF16),
     ]
-    scratch += per_weight(lambda n: (4, 2, 96, n), BF16)
-    scratch += per_weight(lambda n: (2, 2, 96, n), BF16)
-    scratch += per_weight(lambda n: (2, 96, n), BF16)
-    scratch += per_weight(lambda n: (2, 96, n), BF16)
-    scratch += per_weight(lambda n: (4, 48, n), BF16)
-    scratch += per_weight(lambda n: (3, 48, n), BF16)
+    scratch += per_weight(lambda n: (4, 2, 96, n), BF16)[:2]
+    scratch += per_weight(lambda n: (2, 2, 96, n), BF16)[:2]
+    scratch += per_weight(lambda n: (2, 96, n), BF16)[:2]
+    scratch += per_weight(lambda n: (2, 96, n), BF16)[:2]
+    scratch += per_weight(lambda n: (4, 48, n), BF16)[:2]
+    scratch += per_weight(lambda n: (3, 48, n), BF16)[:2]
+    scratch += [pltpu.VMEM((4, 4, 48, KV), BF16), pltpu.VMEM((16, 48, KV), BF16)]
     scratch += per_weight(lambda n: (48, n), F32)
     scratch += per_weight(lambda n: (8, 8, n), F32)
     scratch += per_weight(lambda n: (7, 8, n), F32)
     scratch += [pltpu.SemaphoreType.DMA((len(SLOT),)), pltpu.SemaphoreType.DMA((len(SLOT),))]
-    grad_x, grad_wq, grad_wkv, grad_wo_t = pl.pallas_call(
+    scratch += [pltpu.SemaphoreType.DMA((7,)), pltpu.SemaphoreType.DMA((4,))]
+    results = (
+        jax.ShapeDtypeStruct((ROWS, D), BF16),
+        jax.ShapeDtypeStruct((6, COLS[1]), F32),
+        jax.ShapeDtypeStruct((6, COLS[2]), F32),
+        jax.ShapeDtypeStruct((6, COLS[0]), F32),
+    )
+    outs = pl.pallas_call(
         kernel,
-        out_shape=(
-            jax.ShapeDtypeStruct((ROWS, D), BF16),
-            jax.ShapeDtypeStruct((6, COLS[1]), F32),
-            jax.ShapeDtypeStruct((6, COLS[2]), F32),
-            jax.ShapeDtypeStruct((6, COLS[0]), F32),
-        ),
-        in_specs=[smem] + [vmem] * 6,
-        out_specs=(vmem,) * 4,
+        out_shape=results,
+        in_specs=[hbm] * 7,
+        out_specs=(hbm,) * 4,
         scratch_shapes=scratch,
         compiler_params=pltpu.CompilerParams(
             collective_id=0, has_side_effects=True, vmem_limit_bytes=56 * 1024 * 1024
         ),
-    )(lengths, tokens[0], cotangent[0], gain[None, :], w_q, w_kv, w_o)
+    )(lengths, tokens[0], cotangent[0], gain, w_q, w_kv.T, w_o)
+    grad_x, grad_wq, grad_wkv, grad_wo_t = pl.pallas_call(
+        hand_on,
+        out_shape=results,
+        in_specs=[hbm] * 4,
+        out_specs=(hbm,) * 4,
+        scratch_shapes=[pltpu.VMEM(r.shape, r.dtype) for r in results]
+        + [pltpu.SemaphoreType.DMA((4,)), pltpu.SemaphoreType.DMA((4,))],
+        compiler_params=pltpu.CompilerParams(vmem_limit_bytes=60 * 1024 * 1024),
+    )(*outs)
     return grad_x[None], grad_wq, grad_wkv, grad_wo_t
 
 

time: 82.7 us -> 72.2 us (0.87)
  local copies, waits for them, and re-layouts: 9.38 us -> 0 us
  Pallas kernels: 71.6 us -> 70.7 us
    unnamed x5 -> x0, local copies, waits for them, and re-layouts: 8.08 us -> none
    broadcast_in_dim x1 -> x0, local copies, waits for them, and re-layouts: 1.3 us -> none  [body(): gain[None, :]]
    pallas_call x1 -> x2, Pallas kernels: 71.6 us -> 70.7 us  [the longest x1 68.9 us: body(): pl.pallas_call(kernel, out_shape=results, in_specs=[hbm] * 7, out_specs=(...]
where the time goes in v2:
time: 72.2 us; the launch traced here: 72 us
  Pallas kernels  70.7 us (98%)
  between operations  1.29 us (2%)
    pallas_call x1, Pallas kernels, body(): pl.pallas_call(kernel, out_shape=results, in_specs=[hbm] * 7, out_specs=(...  68.9 us
    pallas_call x1, Pallas kernels, body(): pl.pallas_call(hand_on, out_shape=results, in_specs=[hbm] * 4, out_specs=...  1.82 us

profile of v2, /device:TPU:1, one launch (start us, length us, event | category | flops | bytes accessed | tf_op | source)
XLA Modules:
  0.0 72.0 jit_solution(12399213585876576557)
XLA Ops:
  1.3 68.9 %shard_map.102 = (bf16[128,1536]{1,0:T(8,128)(2,1)}, f32[6,512]{1,0:T(8,128)}, f32[6,320]{1,0:T(8,128)}, f32[6,768]{1,0:T(8,128)}) custom-call(s32[1]{0:T(128)S(6)} %copy.11.len_hbm, bf16[128,1536]{1,0:T(8,128)(2,1)} %bitcast.5, bf16[128,1536]{1,0:T(8,128)(2,1)} %bitcast.6, f32[1536]{0:T(1024)} %gain_hbm.1, bf16[1536,512]{1,0:T(8,128)(2,1)} %wq_hbm.1, ...), custom_call_target="tpu_custom_call" | custom-call | tf_op jit(solution)/shard_map/pallas_call | solution.py:475
  70.2 1.8 %shard_map.103 = (bf16[128,1536]{1,0:T(8,128)(2,1)}, f32[6,512]{1,0:T(8,128)}, f32[6,320]{1,0:T(8,128)}, f32[6,768]{1,0:T(8,128)}) custom-call(bf16[128,1536]{1,0:T(8,128)(2,1)} %get-tuple-element.12.refs_0_, f32[6,512]{1,0:T(8,128)} %get-tuple-element.13.refs_1_, f32[6,320]{1,0:T(8,128)} %get-tuple-element.14.refs_2_, f32[6,768]{1,0:T(8,128)} %get-tuple-element.15.refs_3_), custom_call_target="tpu_custom_call" | custom-call | tf_op jit(solution)/shard_map/pallas_call | solution.py:485

commit v3 on v2

--- a/solution.py
+++ b/solution.py
@@ -24,6 +24,7 @@
 NN = (((1,), (0,)), ((), ()))
 
 COLS = (HEADS * HV, HEADS * HK, KV)
+HALF = (384, 256, 256)
 
 
 def mm(a, b, dims=NN):
@@ -40,7 +41,8 @@
     names += [("rs2", d) for d in range(4)]
     names += [("rsz", d) for d in (1, 2, 3)]
     for w in range(2):
-        names += [("wx1", w, h) for h in (0, 1)]
+        names += [(k, w, h) for k in ("xd", "xf") for h in (0, 1)]
+        names += [("xn", w, h, b) for h in (0, 1) for b in (0, 1)]
         names += [("wx2", w, h) for h in (0, 1)]
         names += [("wy", w, j) for j in (1, 2, 3)]
     names += [("wxy", i, j) for i in range(4) for j in range(4) if i or j]
@@ -60,7 +62,7 @@
     kvt, vals, scores, probs, ub, qt, qts, dat, dats, normed, rscale, dn,
     t, r1, f, r2, zsend, rz,
     nall, call, n2, c2, a2, dq2, dkv2,
-    p0, p1, rx0, rx1, fx0, fx1, sx0, sx1, y0, y1, ry0, ry1,
+    n4, c4, a4, dq4, po0, po1, pf0, pf1, sx0, sx1, y0, y1, ry0, ry1,
     pk, rk, ys0, ys1, ys2, z0, z1, z2, rz0, rz1, rz2,
     ssem, rsem, isem, osem,
 ):
@@ -154,13 +156,29 @@
     for h in range(HEADS):
         da = mm(wo_ref[HV * h : HV * (h + 1), :], cot_ref[...], NT)
         dat[:, lane[h]] = da.astype(BF16)
+    sib = dev(c_=other)
+    nall[...] = normed[...].T.reshape(4, 2, 2, 96, ROWS)
+    sib_n = send(("sib", "n"), nall.at[:, :, other], n2.at[:, :, :, ROWS : 2 * ROWS], sib)
+    n2[:, :, :, 0:ROWS] = nall[:, :, c]
+    call[...] = cot_ref[...].T.reshape(4, 2, 2, 96, ROWS)
+    sib_c = send(("sib", "c"), call.at[:, :, other], c2.at[:, :, :, ROWS : 2 * ROWS], sib)
+    c2[:, :, :, 0:ROWS] = call[:, :, c]
     wait_z(1)
     wait_z(3)
-    nall[...] = normed[...].T.reshape(4, 2, 2, 96, ROWS)
+
+    x1, x3 = dev(x_=xs[1]), dev(x_=xs[3])
+    xd, xf, xn = {}, {}, {}
+
+    def to_x(w, rows, rows4):
+        for h, near, to in ((0, 1, x1), (1, 3, x3)):
+            for b, i in ((0, near), (1, 2)):
+                xn[w, h, b] = send(("xn", w, h, b), rows.at[xs[i], h], rows4.at[h, b], to)
+
+    sib_n.wait_recv()
+    to_x(1, n2, n4)
+    sib_c.wait_recv()
+    to_x(0, c2, c4)
     wait_z(2)
-    sib = dev(c_=other)
-    sib_n = send(("sib", "n"), nall.at[:, :, other], n2.at[:, :, :, ROWS : 2 * ROWS], sib)
-    n2[:, :, :, 0:ROWS] = nall[:, :, c]
 
     loads["len"].wait()
     length = len_ref[0]
@@ -187,9 +205,6 @@
     relay_y(2)
     for d, j in ((0, 1), (1, 1), (2, 3), (3, 3)):
         score(j, d)
-    call[...] = cot_ref[...].T.reshape(4, 2, 2, 96, ROWS)
-    sib_c = send(("sib", "c"), call.at[:, :, other], c2.at[:, :, :, ROWS : 2 * ROWS], sib)
-    c2[:, :, :, 0:ROWS] = call[:, :, c]
     for j, d in ((3, 0), (3, 1), (1, 3), (1, 2)):
         agy[j, d].wait_recv()
         score(j, d)
@@ -215,7 +230,17 @@
     for h in range(HEADS):
         a2[HV * h : HV * (h + 1), 0:ROWS] = att_b[:, lane[h]]
     mine, theirs = slice(0, ROWS), slice(ROWS, 2 * ROWS)
+    def share(w, right, right4):
+        for h, to in ((0, x1), (1, x3)):
+            xd[w, h] = send(("xd", w, h), right.at[:, mine], right4.at[h, :, mine], to)
+
+    def share_on(w, right4):
+        for h in (0, 1):
+            xd[w, h].wait_recv()
+            xf[w, h] = send(("xf", w, h), right4.at[h, :, mine], right4.at[h, :, theirs], sib)
+
     sib_a = send(("sib", "a"), a2.at[:, mine], a2.at[:, theirs], sib)
+    share(0, a2, a4)
 
     def backward(j, dq):
         for d in range(4):
@@ -249,37 +274,29 @@
         if d:
             rsz[d] = send(("rsz", d), zsend.at[d], rz.at[d - 1], dev(zl_=(zl + d) % 4))
 
-    part, rx, fx, sx = (p0, p1), (rx0, rx1), (fx0, fx1), (sx0, sx1)
+    po, pf, sx = (po0, po1), (pf0, pf1), (sx0, sx1)
     yb, ry, ysum = (y0, y1), (ry0, ry1), (ys0, ys1, ys2)
     zb, rzb = (z0, z1, z2), (rz0, rz1, rz2)
     grads, grads_hbm = (gwo_ref, gwq_ref, gwkv_ref), (gwo_hbm, gwq_hbm, gwkv_hbm)
-    x1, x3 = dev(x_=xs[1]), dev(x_=xs[3])
-    wx1, wx2, wy, wz = {}, {}, {}, {}
-
-    def w_part(w, rows, right):
-        for i in (2, 1, 3, 0):
-            left = rows[xs[i]].reshape(192, 2 * ROWS)
-            part[w][i] = mm(left, right[...], NT).reshape(2, 96, COLS[w]).astype(BF16)
-            if i == 1:
-                wx1[w, 0] = send(("wx1", w, 0), part[w].at[1:3, 0], rx[w].at[0], x1)
-            if i == 3:
-                wx1[w, 1] = send(("wx1", w, 1), part[w].at[2:4, 1], rx[w].at[1], x3)
-
-    def w_x2(w):
-        wx1[w, 0].wait_recv()
-        fx[w][0] = (part[w][3, 0].astype(F32) + rx[w][0, 1].astype(F32)).astype(BF16)
-        wx2[w, 0] = send(("wx2", w, 0), fx[w].at[0], sx[w].at[0], x3)
-        wx1[w, 1].wait_recv()
-        fx[w][1] = (part[w][1, 1].astype(F32) + rx[w][1, 0].astype(F32)).astype(BF16)
-        wx2[w, 1] = send(("wx2", w, 1), fx[w].at[1], sx[w].at[1], x1)
+    wx2, wy, wz = {}, {}, {}
+
+    def w_part(w, rows, rows4, right, right4):
+        for h, far, to in ((0, 3, x3), (1, 1, x1)):
+            left = jnp.concatenate([rows[xs[far], h], rows[x, h]], axis=0)
+            xn[w, h, 0].wait_recv()
+            xn[w, h, 1].wait_recv()
+            left4 = jnp.concatenate([rows4[h, 1], rows4[h, 0]], axis=0)
+            xf[w, h].wait_recv()
+            both = mm(left, right[...], NT) + mm(left4, right4[h], NT)
+            pf[w][h] = both[0:96].astype(BF16)
+            wx2[w, h] = send(("wx2", w, h), pf[w].at[h], sx[w].at[h], to)
+            po[w][h] = both[96:192]
 
     def w_y(w):
         sums = []
         for h in (0, 1):
             wx2[w, h].wait_recv()
-            sums.append(
-                part[w][0, h].astype(F32) + rx[w][h, h].astype(F32) + sx[w][h].astype(F32)
-            )
+            sums.append(po[w][h] + sx[w][h].astype(F32))
         for k in range(4):
             rows = slice(24 * k, 24 * (k + 1))
             yb[w][k] = jnp.concatenate([sums[0][rows], sums[1][rows]], axis=0).astype(BF16)
@@ -314,10 +331,14 @@
             for j in (1, 3, 2):
                 wy[w, j].wait_recv()
                 total = total + ry[w][j - 1].astype(F32)
-        ysum[w][...] = total
-        zb[w][...] = jnp.zeros_like(zb[w])
+        ysum[w][0:48, :] = total
+        ysum[w][48:56, :] = jnp.zeros((8, COLS[w]), F32)
         for k in range(8):
-            zb[w][k, 0:6, :] = ysum[w][6 * k : 6 * (k + 1), :]
+            rows = ysum[w][6 * k : 6 * k + 8, :]
+            right = rows[:, HALF[w] :]
+            if right.shape[1] < HALF[w]:
+                right = jnp.concatenate([right, jnp.zeros((8, HALF[w] - right.shape[1]), F32)], axis=1)
+            zb[w][k] = jnp.concatenate([rows[:, : HALF[w]], right], axis=0).astype(BF16)
         for a, b in ((1, 0), (1, 1), (1, 3), (1, 2), (0, 2), (0, 1), (0, 3)):
             zh_, zl_ = (zh + a) % 2, (zl + b) % 4
             wz[w, a, b] = send(
@@ -325,42 +346,42 @@
             )
 
     def w_end(w):
-        total = zb[w][zh * 4 + zl]
+        total = zb[w][zh * 4 + zl].astype(F32)
         for a, b in ((0, 1), (0, 3), (0, 2), (1, 0), (1, 1), (1, 3), (1, 2)):
             wz[w, a, b].wait_recv()
-            total = total + rzb[w][a * 4 + b - 1]
-        grads[w][...] = total[0:6, :]
+            total = total + rzb[w][a * 4 + b - 1].astype(F32)
+        grads[w][:, : HALF[w]] = total[0:6]
+        grads[w][:, HALF[w] :] = total[8:14, : COLS[w] - HALF[w]]
 
     dq = backward(2, jnp.zeros((HK, ALL), F32))
     for d in (1, 2, 0, 3):
         rs_opp(d)
-    sib_c.wait_recv()
-    sib_a.wait_recv()
-    w_part(0, c2, a2)
     dq = backward(1, dq)
     rs_own(1)
     dq = backward(3, dq)
     rs_own(2)
-    rs_fwd(1)
-    rs_fwd(2)
-    rs_own(0)
-    rs_own(3)
     dq = backward(0, dq)
     dq_b = (dq * (inv * SCALE)).astype(BF16)
     for h in range(HEADS):
         dq2[HK * h : HK * (h + 1), mine] = dq_b[:, lane[h]]
     sib_q = send(("sib", "q"), dq2.at[:, mine], dq2.at[:, theirs], sib)
+    share(1, dq2, dq4)
+    rs_fwd(1)
+    rs_fwd(2)
+    rs_own(0)
+    rs_own(3)
+    share_on(0, a4)
     rs_fwd(0)
     rs_fwd(3)
-    sib_n.wait_recv()
-    sib_q.wait_recv()
-    w_part(1, n2, dq2)
+    sib_a.wait_recv()
+    w_part(0, c2, c4, a2, a4)
     rs_sum(1)
     rs_sum(2)
-    w_x2(0)
+    share_on(1, dq4)
+    sib_q.wait_recv()
+    w_part(1, n2, n4, dq2, dq4)
     rs_sum(3)
     rs_sum(0)
-    w_x2(1)
     dqn = jnp.concatenate([dq2[HK * h : HK * (h + 1), mine].T for h in range(HEADS)], axis=1)
     dn[...] = mm(dqn, wq_ref[...], NT)
     w_y(0)
@@ -373,9 +394,9 @@
     sib_kv = send(("sib", "kv"), dkv2.at[:, mine], dkv2.at[:, theirs], sib)
     dkvn = jnp.concatenate([dkv_b[0:HK].T, dkv_b[HK:KV].T], axis=1)
     dn[...] += mm(dkvn, wkv_ref[...])
+    w_y(1)
     sib_kv.wait_recv()
     kv_part()
-    w_y(1)
     xf = tok_ref[...].astype(F32)
     rs = rscale[...]
     gd = gain_ref[...].reshape(1, D) * dn[...]
@@ -454,16 +475,17 @@
         pltpu.VMEM((COLS[1], 2 * ROWS), BF16),
         pltpu.VMEM((COLS[2], 2 * ROWS), BF16),
     ]
-    scratch += per_weight(lambda n: (4, 2, 96, n), BF16)[:2]
-    scratch += per_weight(lambda n: (2, 2, 96, n), BF16)[:2]
+    scratch += [pltpu.VMEM((2, 2, 96, 2 * ROWS), BF16)] * 2
+    scratch += per_weight(lambda n: (2, n, 2 * ROWS), BF16)[:2]
+    scratch += per_weight(lambda n: (2, 96, n), F32)[:2]
     scratch += per_weight(lambda n: (2, 96, n), BF16)[:2]
     scratch += per_weight(lambda n: (2, 96, n), BF16)[:2]
     scratch += per_weight(lambda n: (4, 48, n), BF16)[:2]
     scratch += per_weight(lambda n: (3, 48, n), BF16)[:2]
     scratch += [pltpu.VMEM((4, 4, 48, KV), BF16), pltpu.VMEM((16, 48, KV), BF16)]
-    scratch += per_weight(lambda n: (48, n), F32)
-    scratch += per_weight(lambda n: (8, 8, n), F32)
-    scratch += per_weight(lambda n: (7, 8, n), F32)
+    scratch += per_weight(lambda n: (56, n), F32)
+    scratch += [pltpu.VMEM((8, 16, n), BF16) for n in HALF]
+    scratch += [pltpu.VMEM((7, 16, n), BF16) for n in HALF]
     scratch += [pltpu.SemaphoreType.DMA((len(SLOT),)), pltpu.SemaphoreType.DMA((len(SLOT),))]
     scratch += [pltpu.SemaphoreType.DMA((7,)), pltpu.SemaphoreType.DMA((4,))]
     results = (

time: 72.2 us -> 65.8 us (0.911)
  Pallas kernels: 70.7 us -> 64.3 us
    pallas_call x1, Pallas kernels: 68.9 us -> 62.5 us  [body(): pl.pallas_call(kernel, out_shape=results, in_specs=[hbm] * 7, out_specs=(...]
where the time goes in v3:
time: 65.8 us; the launch traced here: 65.6 us
  Pallas kernels  64.3 us (98%)
  between operations  1.29 us (2%)
    pallas_call x1, Pallas kernels, body(): pl.pallas_call(kernel, out_shape=results, in_specs=[hbm] * 7, out_specs=(...  62.5 us
    pallas_call x1, Pallas kernels, body(): pl.pallas_call(hand_on, out_shape=results, in_specs=[hbm] * 4, out_specs=...  1.82 us

profile of v3, /device:TPU:1, one launch (start us, length us, event | category | flops | bytes accessed | tf_op | source)
XLA Modules:
  0.0 65.6 jit_solution(15485085690621465524)
XLA Ops:
  1.3 62.5 %shard_map.102 = (bf16[128,1536]{1,0:T(8,128)(2,1)}, f32[6,512]{1,0:T(8,128)}, f32[6,320]{1,0:T(8,128)}, f32[6,768]{1,0:T(8,128)}) custom-call(s32[1]{0:T(128)S(6)} %copy.11.len_hbm, bf16[128,1536]{1,0:T(8,128)(2,1)} %bitcast.5, bf16[128,1536]{1,0:T(8,128)(2,1)} %bitcast.6, f32[1536]{0:T(1024)} %gain_hbm.1, bf16[1536,512]{1,0:T(8,128)(2,1)} %wq_hbm.1, ...), custom_call_target="tpu_custom_call" | custom-call | tf_op jit(solution)/shard_map/pallas_call | solution.py:497
  63.8 1.8 %shard_map.103 = (bf16[128,1536]{1,0:T(8,128)(2,1)}, f32[6,512]{1,0:T(8,128)}, f32[6,320]{1,0:T(8,128)}, f32[6,768]{1,0:T(8,128)}) custom-call(bf16[128,1536]{1,0:T(8,128)(2,1)} %get-tuple-element.12.refs_0_, f32[6,512]{1,0:T(8,128)} %get-tuple-element.13.refs_1_, f32[6,320]{1,0:T(8,128)} %get-tuple-element.14.refs_2_, f32[6,768]{1,0:T(8,128)} %get-tuple-element.15.refs_3_), custom_call_target="tpu_custom_call" | custom-call | tf_op jit(solution)/shard_map/pallas_call | solution.py:507

commit v4 on v3

--- a/solution.py
+++ b/solution.py
@@ -33,9 +33,9 @@
 
 def make_slots():
     names = []
-    names += [("agz", d) for d in (1, 2, 3)]
-    names += [("agy", j, d) for j in (1, 3) for d in range(4)]
-    names += [("agr", d) for d in range(4)]
+    names += [("agz", d, p) for d in (1, 2, 3) for p in (0, 1)]
+    names += [("agy", j, d, p) for j in (1, 3) for d in range(4) for p in (0, 1)]
+    names += [("agr", d, p) for d in range(4) for p in (0, 1)]
     names += [("sib", k) for k in ("n", "c", "a", "q", "kv")]
     names += [("rs1", d, k) for d in range(4) for k in (0, 1)]
     names += [("rs2", d) for d in range(4)]
@@ -126,25 +126,37 @@
     agz, agy, agr = {}, {}, {}
     lane = [slice(ROWS * d, ROWS * (d + 1)) for d in range(4)]
 
-    def to_y(d):
+    parts = (slice(0, HK), slice(HK, KV))
+
+    def to_y(d, p):
         for j in (1, 3):
-            agy[j, d] = send(("agy", j, d), kvt.at[0, :, lane[d]], kvt.at[j, :, lane[d]], dev(y_=ys[j]))
+            agy[j, d, p] = send(
+                ("agy", j, d, p), kvt.at[0, parts[p], lane[d]], kvt.at[j, parts[p], lane[d]], dev(y_=ys[j])
+            )
 
     def to_z(d):
-        agz[d] = send(("agz", d), kvt.at[0, :, lane[0]], kvt.at[0, :, lane[d]], dev(zl_=(zl + 4 - d) % 4))
+        for p in (0, 1):
+            agz[d, p] = send(
+                ("agz", d, p), kvt.at[0, parts[p], lane[0]], kvt.at[0, parts[p], lane[d]], dev(zl_=(zl + 4 - d) % 4)
+            )
 
     def relay_y(d):
         j, to = ((1, 3), (1, 3), (3, 1), (3, 1))[d]
-        agy[j, d].wait_recv()
-        agr[d] = send(("agr", d), kvt.at[j, :, lane[d]], kvt.at[2, :, lane[d]], dev(y_=ys[to]))
+        for p in (0, 1):
+            agy[j, d, p].wait_recv()
+            agr[d, p] = send(
+                ("agr", d, p), kvt.at[j, parts[p], lane[d]], kvt.at[2, parts[p], lane[d]], dev(y_=ys[to])
+            )
 
     def wait_z(d):
-        agz[d].wait_recv()
-        to_y(d)
+        for p in (0, 1):
+            agz[d, p].wait_recv()
+            to_y(d, p)
 
     to_z(1)
     to_z(3)
-    to_y(0)
+    to_y(0, 0)
+    to_y(0, 1)
     to_z(2)
     loads["wq"].wait()
     q = mm(normed[...], wq_ref[...])
@@ -206,10 +218,12 @@
     for d, j in ((0, 1), (1, 1), (2, 3), (3, 3)):
         score(j, d)
     for j, d in ((3, 0), (3, 1), (1, 3), (1, 2)):
-        agy[j, d].wait_recv()
+        for p in (0, 1):
+            agy[j, d, p].wait_recv()
         score(j, d)
     for d in (0, 1, 3, 2):
-        agr[d].wait_recv()
+        for p in (0, 1):
+            agr[d, p].wait_recv()
         score(2, d)
 
     top = jnp.max(tops[0], axis=0, keepdims=True)
@@ -397,6 +411,8 @@
     w_y(1)
     sib_kv.wait_recv()
     kv_part()
+    w_z(0)
+    w_z(1)
     xf = tok_ref[...].astype(F32)
     rs = rscale[...]
     gd = gain_ref[...].reshape(1, D) * dn[...]
@@ -405,8 +421,6 @@
     gtok_ref[...] = out.astype(BF16)
     stores = [pltpu.make_async_copy(gtok_ref, gtok_hbm, osem.at[3])]
     stores[0].start()
-    w_z(0)
-    w_z(1)
     w_z(2)
     for w in range(3):
         w_end(w)

time: 65.8 us -> 65.6 us (level)
  no operation moved by 1% of the time
where the time goes in v4:
time: 65.6 us; the launch traced here: 65.4 us
  Pallas kernels  64.2 us (98%)
  between operations  1.29 us (2%)
    pallas_call x1, Pallas kernels, body(): pl.pallas_call(kernel, out_shape=results, in_specs=[hbm] * 7, out_specs=(...  62.3 us
    pallas_call x1, Pallas kernels, body(): pl.pallas_call(hand_on, out_shape=results, in_specs=[hbm] * 4, out_specs=...  1.82 us

profile of v4, /device:TPU:1, one launch (start us, length us, event | category | flops | bytes accessed | tf_op | source)
XLA Modules:
  0.0 65.4 jit_solution(4287241384315221573)
XLA Ops:
  1.3 62.3 %shard_map.102 = (bf16[128,1536]{1,0:T(8,128)(2,1)}, f32[6,512]{1,0:T(8,128)}, f32[6,320]{1,0:T(8,128)}, f32[6,768]{1,0:T(8,128)}) custom-call(s32[1]{0:T(128)S(6)} %copy.11.len_hbm, bf16[128,1536]{1,0:T(8,128)(2,1)} %bitcast.5, bf16[128,1536]{1,0:T(8,128)(2,1)} %bitcast.6, f32[1536]{0:T(1024)} %gain_hbm.1, bf16[1536,512]{1,0:T(8,128)(2,1)} %wq_hbm.1, ...), custom_call_target="tpu_custom_call" | custom-call | tf_op jit(solution)/shard_map/pallas_call | solution.py:511
  63.6 1.8 %shard_map.103 = (bf16[128,1536]{1,0:T(8,128)(2,1)}, f32[6,512]{1,0:T(8,128)}, f32[6,320]{1,0:T(8,128)}, f32[6,768]{1,0:T(8,128)}) custom-call(bf16[128,1536]{1,0:T(8,128)(2,1)} %get-tuple-element.12.refs_0_, f32[6,512]{1,0:T(8,128)} %get-tuple-element.13.refs_1_, f32[6,320]{1,0:T(8,128)} %get-tuple-element.14.refs_2_, f32[6,768]{1,0:T(8,128)} %get-tuple-element.15.refs_3_), custom_call_target="tpu_custom_call" | custom-call | tf_op jit(solution)/shard_map/pallas_call | solution.py:521
